TPU v7x, 32 devices: a whole 2x2x4 slice. The times are simulated.
32 devices in a mesh: groups: 1, lon: 32 (over z, y, x, core).
Axes of the slice: x: 2, y: 2, z: 4, core: 2. Of those that a mesh axis runs over, the one named last changes fastest.
Arguments:
- tokens: bfloat16 [512, 32, 1536], P(('groups', 'lon')), may hold values from -40 to 40, as said below
- qkv: bfloat16 [3, 512, 32, 1536], P(None, ('groups', 'lon')), may hold values from -6 to 6
- bias_table: float32 [24, 225], replicated, may hold values from -3 to 3
- out_weight: bfloat16 [1536, 1536], replicated, may hold values from -0.15625 to 0.15625
- norm_gain: float32 [1536], replicated, may hold values from 0.25 to 1.75
- router: bfloat16 [1536, 32], replicated, may hold values from -0.15625 to 0.15625
- expert_ids: int32 [512, 32, 1], P(('groups', 'lon')), may hold values from 0 to 31; in each aligned block of 512 rows (0 to 511, 512 to 1023, ..., all dimensions but the last counted through in order) at most 32 rows name the same one
- slot_expert: int32 [32], replicated, may hold values from 0 to 31, each once
- up_weight: bfloat16 [32, 1536, 1024], P('lon'), may hold values from -0.15625 to 0.15625
- down_weight: bfloat16 [32, 1024, 1536], P('lon'), may hold values from -0.1875 to 0.1875
Outputs:
- blended: bfloat16 [512, 32, 1536], P(('groups', 'lon'))
Inputs may be any that keep to these rules, and one draw needn't show every extreme that they name: tokens: entries of a normal or uniform law times token and feature scales. `expert_ids`: among the 512 tokens of one device (columns of one device, all latitude rows) at most 32 name the same expert. `slot_expert`: each expert stands in exactly one slot; slot s lives on device s of lon.
All inputs are finite; a program needn't handle non-finite values.
Results may differ from a plain program's by a relative error of at most 0.0051.
Values may be sent and summed in bfloat16 or wider, within the bound.
A program may use at most 128 MiB of HBM per device.

v0:
```python
import math

import jax
import jax.numpy as jnp
import numpy as np
from jax import lax
from jax.sharding import PartitionSpec as P

HEAD = 64
WIN = 8
SHIFT = 4


def from_behind(value, axis, steps):
    count = lax.axis_size(axis)
    pairs = [(source, (source + steps) % count) for source in range(count)]
    return lax.ppermute(value, axis, pairs)


def bias_index():
    lon_offset = np.arange(WIN * WIN) // WIN
    lat_offset = np.arange(WIN * WIN) % WIN
    along_lon = lon_offset[:, None] - lon_offset[None, :] + WIN - 1
    along_lat = lat_offset[:, None] - lat_offset[None, :] + WIN - 1
    return along_lon * (2 * WIN - 1) + along_lat


def region_labels(lat_count):
    rolled_rows = jnp.arange(lat_count)
    return jnp.where(
        rolled_rows < lat_count - WIN, 0, jnp.where(rolled_rows < lat_count - SHIFT, 1, 2)
    ).astype(jnp.int32)


def to_windows(grid):
    lon_count, lat_count, features = grid.shape
    blocks = grid.reshape(lon_count // WIN, WIN, lat_count // WIN, WIN, features).transpose(
        0, 2, 1, 3, 4
    )
    return blocks.reshape(lon_count // WIN * (lat_count // WIN), WIN * WIN, features)


def from_windows(windows, lon_count, lat_count):
    features = windows.shape[-1]
    blocks = windows.reshape(lon_count // WIN, lat_count // WIN, WIN, WIN, features).transpose(
        0, 2, 1, 3, 4
    )
    return blocks.reshape(lon_count, lat_count, features)


def attend(queries, keys_win, values, labels, bias_table):
    win_count = queries.shape[0]
    head_count = queries.shape[-1] // HEAD
    query_heads = queries.reshape(win_count, WIN * WIN, head_count, HEAD)
    key_heads = keys_win.reshape(win_count, WIN * WIN, head_count, HEAD)
    value_heads = values.reshape(win_count, WIN * WIN, head_count, HEAD)
    scores = jnp.einsum(
        "wqhd,wkhd->whqk", query_heads, key_heads, preferred_element_type=jnp.float32
    ) / math.sqrt(HEAD)
    scores = scores + bias_table[:, bias_index()][None]
    allowed = labels[:, :, None] == labels[:, None, :]
    scores = jnp.where(allowed[:, None], scores, -1000000000.0)
    highest = jnp.max(scores, axis=-1, keepdims=True)
    weights = jnp.exp(scores - highest)
    weights_bf = (weights / jnp.sum(weights, axis=-1, keepdims=True)).astype(jnp.bfloat16)
    attended = jnp.einsum(
        "whqk,wkhd->wqhd", weights_bf, value_heads, preferred_element_type=jnp.float32
    )
    return attended.reshape(win_count, WIN * WIN, head_count * HEAD).astype(jnp.bfloat16)


def window_pass(stacked, bias_table):
    lon_count = stacked.shape[1]
    lat_count = stacked.shape[2]
    label_grid = jnp.broadcast_to(
        region_labels(lat_count)[None, :, None], (lon_count, lat_count, 1)
    )
    labels = to_windows(label_grid)[:, :, 0]
    attended = attend(
        to_windows(stacked[0]), to_windows(stacked[1]), to_windows(stacked[2]), labels, bias_table
    )
    return from_windows(attended, lon_count, lat_count)


def expert_apply(rows_in, up_local, down_local):
    features = rows_in.shape[-1]
    flat_rows = rows_in.reshape(-1, features)
    hidden = jax.nn.gelu(jnp.dot(flat_rows, up_local, preferred_element_type=jnp.float32)).astype(
        jnp.bfloat16
    )
    result = jnp.dot(hidden, down_local, preferred_element_type=jnp.float32).astype(jnp.bfloat16)
    return result.reshape(rows_in.shape)


def local(
    tokens,
    qkv,
    bias_table,
    out_weight,
    norm_gain,
    router,
    expert_ids,
    slot_expert,
    up_weight,
    down_weight,
):
    columns = tokens.shape[0]
    lat_count = tokens.shape[1]
    features = tokens.shape[2]
    rolled = jnp.roll(qkv, -SHIFT, axis=2)
    nearby = from_behind(rolled[:, :SHIFT], "lon", -1)
    extended = jnp.concatenate([rolled[:, SHIFT:], nearby], axis=1)
    computed = window_pass(extended, bias_table)
    returned_rim = from_behind(computed[columns - SHIFT :], "lon", 1)
    attended = jnp.concatenate([returned_rim, computed[: columns - SHIFT]], axis=0)
    attended = jnp.roll(attended, SHIFT, axis=1)
    projected = jnp.dot(
        attended.reshape(-1, features), out_weight, preferred_element_type=jnp.float32
    )
    resid = (tokens.reshape(-1, features).astype(jnp.float32) + projected).astype(jnp.bfloat16)
    resid_f = resid.astype(jnp.float32)
    scale = lax.rsqrt(jnp.mean(resid_f * resid_f, axis=-1, keepdims=True) + 1e-05)
    normed = (resid_f * scale * norm_gain[None, :]).astype(jnp.bfloat16)
    peers = lax.axis_size("lon")
    experts = up_weight.shape[0] * peers
    token_count = columns * lat_count
    capacity = 2 * token_count // experts
    logits = jnp.dot(normed, router, preferred_element_type=jnp.float32)
    chosen = expert_ids.reshape(-1)
    expert_range = jnp.arange(experts, dtype=jnp.int32)
    chosen_hot = chosen[:, None] == expert_range[None, :]
    gate = jax.nn.sigmoid(jnp.sum(jnp.where(chosen_hot, logits, 0.0), axis=-1))
    slot_of = jnp.sum(
        jnp.where(slot_expert[None, :] == expert_range[:, None], expert_range[None, :], 0), axis=1
    )
    target = jnp.sum(jnp.where(chosen_hot, slot_of[None, :], 0), axis=1)
    target_hot = (target[:, None] == jnp.arange(peers, dtype=jnp.int32)[None, :]).astype(jnp.int32)
    earlier = jnp.cumsum(target_hot, axis=0) - target_hot
    position = target * capacity + jnp.sum(earlier * target_hot, axis=1)
    selector = (position[None, :] == jnp.arange(peers * capacity, dtype=jnp.int32)[:, None]).astype(
        jnp.bfloat16
    )
    outgoing = jnp.dot(selector, normed, preferred_element_type=jnp.float32).astype(jnp.bfloat16)
    outgoing = outgoing.reshape(peers, capacity, features)
    up_local = up_weight[0]
    down_local = down_weight[0]
    incoming = lax.all_to_all(outgoing, "lon", split_axis=0, concat_axis=0, tiled=True)
    answers = expert_apply(incoming, up_local, down_local)
    returned = lax.all_to_all(answers, "lon", split_axis=0, concat_axis=0, tiled=True)
    gathered = jnp.einsum(
        "st,sd->td", selector, returned.reshape(-1, features), preferred_element_type=jnp.float32
    )
    blended = resid_f + gate[:, None] * gathered
    return blended.astype(jnp.bfloat16).reshape(columns, lat_count, features)


def solution(mesh):
    in_specs = (
        P(("groups", "lon"), None, None),
        P(None, ("groups", "lon"), None, None),
        P(),
        P(),
        P(),
        P(),
        P(("groups", "lon"), None, None),
        P(),
        P("lon", None, None),
        P("lon", None, None),
    )
    out_specs = P(("groups", "lon"), None, None)
    return jax.shard_map(local, mesh=mesh, in_specs=in_specs, out_specs=out_specs, check_vma=False)
```

profile of v0, /device:TPU:9, one launch (start us, length us, event | category | flops | bytes accessed | tf_op | source)
XLA Modules:
  0.0 268.1 jit_solution(2486887966613087874)
XLA Ops:
  0.0 5.0 %slice.43 = bf16[3,16,28,1536]{3,2,1,0:T(8,128)(2,1)S(1)} slice(bf16[3,16,32,1536]{3,2,1,0:T(8,128)(2,1)} %param.13), slice={[0:3], [0:16], [4:32], [0:1536]} | slice | bytes 8257536 | tf_op jit(solution)/shard_map/jit(_roll_static)/slice | solution.py:110
  5.0 2.3 slice.44
  7.4 1.2 pad_maximum_fusion.3
  9.4 14.1 %gather_fusion = f32[4096,24]{1,0:T(8,128)} fusion(f32[24,225]{0,1:T(8,128)S(1)} %copy.35, s32[4096]{0:T(1024)S(1)} %broadcast_clamp_fusion), kind=kCustom, calls=%fused_computation | custom fusion | bytes 802816 | tf_op jit(solution)/shard_map/gather | solution.py:60
  23.4 3.7 %copy.36 = f32[64,64,24]{0,1,2:T(8,128)} copy(f32[64,64,24]{2,1,0:T(8,128)} %bitcast.81) | data formatting | bytes 786432 | tf_op jit(solution)/shard_map/gather | solution.py:60
  28.6 1.2 reduce-window.6
  29.9 2.6 fusion.10
  32.5 3.0 %fusion.37 = (bf16[1,16,32,1536]{3,2,1,0:T(8,128)(2,1)}, bf16[1,16,32,1536]{3,2,1,0:T(8,128)(2,1)}, bf16[1,16,32,1536]{3,2,1,0:T(8,128)(2,1)S(1)}) fusion(bf16[3,12,32,1536]{3,2,1,0:T(8,128)(2,1)S(1)} %fusion.10, bf16[3,4,32,1536]{3,2,1,0:T(8,128)(2,1)} %collective-permute-done), kind=kLoop, calls=%fused_computation.54 | loop fusion | flops 2359296 | bytes 9437184 | tf_op jit(solution)/shard_map/concatenate | solution.py:112
  35.6 1.3 copy.57
  36.9 5.1 %reshape_reshape.10 = bf16[8,64,24,64]{3,2,1,0:T(8,128)(2,1)} reshape(bf16[2,4,8,8,1536]{4,3,2,1,0:T(8,128)(2,1)} %bitcast.77) | data formatting | bytes 3145728 | tf_op jit(solution)/shard_map/reshape;reshape | solution.py:54
  41.9 2.7 %copy.56 = bf16[2,8,4,8,1536]{4,3,1,2,0:T(8,128)(2,1)} copy(bf16[2,8,4,8,1536]{4,3,2,1,0:T(8,128)(2,1)} %bitcast.75) | data formatting | bytes 3145728 | tf_op jit(solution)/shard_map/reshape;squeeze | solution.py:37
  44.6 5.1 %reshape_reshape.11 = bf16[8,64,24,64]{3,2,1,0:T(8,128)(2,1)} reshape(bf16[2,4,8,8,1536]{4,3,2,1,0:T(8,128)(2,1)} %bitcast.78) | data formatting | bytes 3145728 | tf_op jit(solution)/shard_map/reshape;reshape | solution.py:55
  49.7 2.7 %copy.58 = bf16[2,8,4,8,1536]{4,3,1,2,0:T(8,128)(2,1)} copy(bf16[2,8,4,8,1536]{4,3,2,1,0:T(8,128)(2,1)} %bitcast.74) | data formatting | bytes 3145728 | tf_op jit(solution)/shard_map/reshape;squeeze | solution.py:37
  52.4 5.1 %reshape_reshape.9 = bf16[8,64,24,64]{3,2,1,0:T(8,128)(2,1)} reshape(bf16[2,4,8,8,1536]{4,3,2,1,0:T(8,128)(2,1)} %bitcast.79) | data formatting | bytes 3145728 | tf_op jit(solution)/shard_map/reshape;reshape | solution.py:56
  57.5 4.7 %fusion.20 = f32[8,24,64,64]{2,3,1,0:T(8,128)S(1)} fusion(bf16[8,64,24,64]{3,2,1,0:T(8,128)(2,1)} %reshape_reshape.11, bf16[8,64,24,64]{3,2,1,0:T(8,128)(2,1)} %reshape_reshape.10), kind=kOutput, calls=%fused_computation.38 | convolution fusion | flops 100663296 | bytes 6291456 | tf_op jit(solution)/shard_map/wqhd,wkhd->whqk/dot_general | solution.py:57
  62.2 2.2 fusion.60
  64.4 2.9 %convert_bitcast_fusion = bf16[8,64,24,64]{1,3,2,0:T(8,128)(2,1)} fusion(f32[8,24,64,64]{2,3,1,0:T(8,128)S(1)} %get-tuple-element.9, f32[8,24,64]{2,1,0:T(8,128)S(1)} %get-tuple-element.8, bf16[8,64,24,64]{3,2,1,0:T(8,128)(2,1)S(1)} %copy-done.4), kind=kOutput, calls=%fused_computation.41 | convolution fusion | flops 103022592 | bytes 6340608 | tf_op jit(solution)/shard_map/whqk,wkhd->wqhd/dot_general | solution.py:66
  67.3 4.9 %copy.39 = bf16[8,64,24,64]{3,2,1,0:T(8,128)(2,1)} copy(bf16[8,64,24,64]{1,3,2,0:T(8,128)(2,1)} %convert_bitcast_fusion) | data formatting | bytes 3145728 | tf_op jit(solution)/shard_map/convert_element_type | solution.py:69
  72.2 5.3 %convert_element_type.53 = bf16[2,4,8,8,1536]{4,3,2,1,0:T(8,128)(2,1)} reshape(bf16[8,64,24,64]{3,2,1,0:T(8,128)(2,1)} %copy.39) | data formatting | bytes 3145728 | tf_op jit(solution)/shard_map/convert_element_type | solution.py:69
  77.6 1.6 copy.40
  79.1 1.1 copy-done.2
  82.5 1.5 slice.65
  84.0 3.2 %collective-permute-done.1 = bf16[4,32,1536]{2,1,0:T(8,128)(2,1)} collective-permute-done((bf16[4,32,1536]{2,1,0:T(8,128)(2,1)}, bf16[4,32,1536]{2,1,0:T(8,128)(2,1)}, u32[]{:S(2)}, u32[]{:S(2)}) %collective-permute-start.1) | collective-permute-done | bytes 393248 | tf_op jit(solution)/shard_map/ppermute | solution.py:17
  87.2 1.6 fusion.38
  88.8 5.1 %fusion.11 = (f32[512]{0:T(512)S(1)}, bf16[512,1536]{1,0:T(8,128)(2,1)S(1)}) fusion(bf16[512,1536]{1,0:T(8,128)(2,1)S(1)} %bitcast.85, bf16[1536,1536]{1,0:T(8,128)(2,1)} %param.15, bf16[512,1536]{1,0:T(8,128)(2,1)S(1)} %bitcast.88), kind=kOutput, calls=%fused_computation.29 | convolution fusion | flops 2420637184 | bytes 9439232 | tf_op jit(solution)/shard_map/dot_general | solution.py:117
  94.0 2.0 convolution_convert_fusion
  96.0 82.4 %all_to_all.10 = bf16[32,32,1536]{2,1,0:T(8,128)(2,1)} all-to-all(bf16[32,32,1536]{2,1,0:T(8,128)(2,1)S(1)} %bitcast.84), channel_id=1, replica_groups=mesh['groups'=1,'lon'=32] {'lon'}, dimensions={0} | all-to-all | bytes 6291456 | tf_op jit(solution)/shard_map/all_to_all | solution.py:147
  178.4 10.8 %convolution_convert_fusion.1 = bf16[1024,1536]{1,0:T(8,128)(2,1)} fusion(bf16[1,1024,1536]{2,1,0:T(8,128)(2,1)S(1)} %copy-done, bf16[1024,1536]{1,0:T(8,128)(2,1)} %bitcast.83, bf16[1,1536,1024]{2,1,0:T(8,128)(2,1)} %param.20), kind=kOutput, calls=%fused_computation.25 | convolution fusion | flops 6453460992 | bytes 12582912 | tf_op jit(solution)/shard_map/dot_general | solution.py:91
  189.1 4.6 %all-to-all-start.1 = ((bf16[32,32,1536]{2,1,0:T(8,128)(2,1)}), bf16[32,32,1536]{2,1,0:T(8,128)(2,1)}, u32[]{:S(2)}, u32[]{:S(2)}) async-start(bf16[32,32,1536]{2,1,0:T(8,128)(2,1)} %bitcast.82), calls=%async_computation.1 | async-start | bytes 6291456 | tf_op jit(solution)/shard_map/all_to_all | solution.py:149
  193.8 2.1 fusion.39
  195.9 66.9 %all-to-all-done.1 = bf16[32,32,1536]{2,1,0:T(8,128)(2,1)} async-done(((bf16[32,32,1536]{2,1,0:T(8,128)(2,1)}), bf16[32,32,1536]{2,1,0:T(8,128)(2,1)}, u32[]{:S(2)}, u32[]{:S(2)}) %all-to-all-start.1) | async-done | bytes 3145760 | tf_op jit(solution)/shard_map/all_to_all | solution.py:149
  262.7 5.4 %fusion.14 = bf16[512,1536]{1,0:T(8,128)(2,1)} fusion(bf16[512,1536]{1,0:T(8,128)(2,1)} %copy-done.13, bf16[1024,1536]{1,0:T(8,128)(2,1)} %bitcast.20, f32[512]{0:T(512)S(1)} %add_divide_fusion, s32[512]{0:T(512)S(1)} %multiply_add_fusion), kind=kOutput, calls=%fused_computation.32 | convolution fusion | flops 1614282752 | bytes 6295552 | tf_op jit(solution)/shard_map/st,sd->td/dot_general | solution.py:150
  (50 shorter events, 4.7 us)
Async XLA Ops:
  0.0 178.4 %copy-start = (bf16[1,1024,1536]{2,1,0:T(8,128)(2,1)S(1)}, bf16[1,1024,1536]{2,1,0:T(8,128)(2,1)}, u32[]{:S(2)}) copy-start(bf16[1,1024,1536]{2,1,0:T(8,128)(2,1)} %param.21) | copy-start | bytes 9437188
  5.0 3.5 %copy-start.1 = (bf16[3,16,28,1536]{3,2,1,0:T(8,128)(2,1)}, bf16[3,16,28,1536]{3,2,1,0:T(8,128)(2,1)S(1)}, u32[]{:S(2)}) copy-start(bf16[3,16,28,1536]{3,2,1,0:T(8,128)(2,1)S(1)} %slice.43) | copy-start | bytes 12386308
  7.3 1.2 copy-start.3
  7.3 1.9 copy-start.7
  7.4 1.9 copy-start.6
  8.6 24.0 %collective-permute-start = (bf16[3,4,32,1536]{3,2,1,0:T(8,128)(2,1)}, bf16[3,4,32,1536]{3,2,1,0:T(8,128)(2,1)}, u32[]{:S(2)}, u32[]{:S(2)}) collective-permute-start(bf16[3,4,32,1536]{3,2,1,0:T(8,128)(2,1)} %pad_maximum_fusion.3), channel_id=1, source_target_pairs={{0,31},{1,0},{2,1},{3,2},{4,3},{5,4},{6,5},{7,6},{8,7},{9,8},{10,9... | collective-permute-start | bytes 3538952 | tf_op jit(solution)/shard_map/ppermute | solution.py:17
  9.3 18.4 %copy-start.8 = (s32[16,32,1]{1,2,0:T(1,128)S(1)}, s32[16,32,1]{1,2,0:T(1,128)}, u32[]{:S(2)}) copy-start(s32[16,32,1]{1,2,0:T(1,128)} %param.18) | copy-start | bytes 6148
  9.4 19.1 %copy-start.12 = (s32[32]{0:T(128)S(1)}, s32[32]{0:T(128)}, u32[]{:S(2)}) copy-start(s32[32]{0:T(128)} %param.19) | copy-start | bytes 388
  57.5 4.7 %copy-start.5 = (f32[64,64,24]{0,1,2:T(8,128)S(1)}, f32[64,64,24]{0,1,2:T(8,128)}, u32[]{:S(2)}) copy-start(f32[64,64,24]{0,1,2:T(8,128)} %copy.36) | copy-start | bytes 1179652
  62.2 2.2 copy-start.4
  79.1 1.1 copy-start.2
  81.0 6.2 %collective-permute-start.1 = (bf16[4,32,1536]{2,1,0:T(8,128)(2,1)}, bf16[4,32,1536]{2,1,0:T(8,128)(2,1)}, u32[]{:S(2)}, u32[]{:S(2)}) collective-permute-start(bf16[4,32,1536]{2,1,0:T(8,128)(2,1)} %slice.64), channel_id=1, source_target_pairs={{0,1},{1,2},{2,3},{3,4},{4,5},{5,6},{6,7},{7,8},{8,9},{9,10},{10,1... | collective-permute-start | bytes 1179656 | tf_op jit(solution)/shard_map/ppermute | solution.py:17
  82.4 6.4 %copy-start.9 = (bf16[16,32,1536]{2,1,0:T(8,128)(2,1)S(1)}, bf16[16,32,1536]{2,1,0:T(8,128)(2,1)}, u32[]{:S(2)}) copy-start(bf16[16,32,1536]{2,1,0:T(8,128)(2,1)} %param.12) | copy-start | bytes 4718596
  88.8 5.2 %copy-start.11 = (f32[1536]{0:T(1024)S(1)}, f32[1536]{0:T(1024)}, u32[]{:S(2)}) copy-start(f32[1536]{0:T(1024)} %param.16) | copy-start | bytes 18436
  94.0 2.0 copy-start.13
  189.1 4.6 %copy-start.10 = (bf16[1536,32]{0,1:T(8,128)(2,1)S(1)}, bf16[1536,32]{0,1:T(8,128)(2,1)}, u32[]{:S(2)}) copy-start(bf16[1536,32]{0,1:T(8,128)(2,1)} %param.17) | copy-start | bytes 294916
  189.1 73.6 %all-to-all-start.1 = ((bf16[32,32,1536]{2,1,0:T(8,128)(2,1)}), bf16[32,32,1536]{2,1,0:T(8,128)(2,1)}, u32[]{:S(2)}, u32[]{:S(2)}) async-start(bf16[32,32,1536]{2,1,0:T(8,128)(2,1)} %bitcast.82), calls=%async_computation.1 | async-start | bytes 6291456 | tf_op jit(solution)/shard_map/all_to_all | solution.py:149
where the time goes:
time: 273 us; the launch traced here: 268 us
  blocking collectives  82.4 us (30%)
  waiting for transfers between devices  70.1 us (26%)
  local copies, waits for them, and re-layouts  63.2 us (23%)
  matrix products  33 us (12%)
  other arithmetic  12.9 us (5%)
  starting transfers between devices  6.39 us (2%)
    all_to_all x1, blocking collectives, local(): lax.all_to_all(outgoing, 'lon', split_axis=0, concat_axis=0, tiled=True)  82.4 us
    all_to_all x1, waiting for transfers between devices, local(): lax.all_to_all(answers, 'lon', split_axis=0, concat_axis=0, tiled=True)  66.9 us
    gather x2, local copies, waits for them, and re-layouts, attend(): scores = scores + bias_table[:, bias_index()][None]  17.8 us
    dot_general x1, matrix products, expert_apply(): jnp.dot(hidden, down_local, preferred_element_type=jnp.float32)  10.8 us
    convert_element_type x2, local copies, waits for them, and re-layouts, attend(): attended.reshape(win_count, WIN * WIN, head_count * HEAD)  10.2 us
    slice x2, local copies, waits for them, and re-layouts, local(): rolled = jnp.roll(qkv, -SHIFT, axis=2)  7.31 us
    another operation x3, local copies, waits for them, and re-layouts, to_windows(): grid.reshape(lon_count // WIN, WIN, lat_count // WIN, WIN, features)  6.73 us
  transfers between devices with their start and end apart: 3, of which 2 were waited for; matrix products, arithmetic and copies ran while one was open for 10% of the time, Pallas kernels for 0%

commit v1 on v0

v1 whole, which is shorter than its diff:
```python
import functools

import jax
import jax.numpy as jnp
import numpy as np
from jax import lax
from jax.experimental import pallas as pl
from jax.experimental.pallas import tpu as pltpu
from jax.sharding import PartitionSpec as P

HEAD = 64
WIN = 8
SHIFT = 4
GROUP = 4
WIDE = GROUP * HEAD
F32 = jnp.float32
BF16 = jnp.bfloat16


def from_behind(value, axis, steps):
    count = lax.axis_size(axis)
    pairs = [(source, (source + steps) % count) for source in range(count)]
    return lax.ppermute(value, axis, pairs)


def bias_spread():
    side = 2 * WIN - 1
    spread = np.zeros((side * side, WIN, 128), np.float32)
    for row in range(WIN):
        for block in range(side):
            for col in range(WIN):
                entry = (side - 1 - block) * side + row - col + WIN - 1
                spread[entry, row, block * WIN + col] = 1.0
    return spread.reshape(side * side, WIN * 128)


def shift_up(grid):
    grid = grid.astype(F32)
    return jnp.concatenate([grid[:, SHIFT:], grid[:, :SHIFT]], axis=1)


def front_kernel(
    q_ref, k_ref, v_ref, prev_ref, next_ref, strip_ref, weight_ref, tokens_ref, gain_ref,
    router_ref, chosen_ref, resid_ref, normed_ref, gate_ref, total, rolled,
):
    step = pl.program_id(0)
    columns, lats = q_ref.shape[1], q_ref.shape[2]
    lat_windows = lats // WIN
    q = shift_up(q_ref[0]) * (1.0 / 8.0)
    k = shift_up(k_ref[0])
    v = shift_up(v_ref[0])
    prev_k, prev_v = shift_up(prev_ref[0]), shift_up(prev_ref[1])
    next_k, next_v = shift_up(next_ref[0]), shift_up(next_ref[1])

    heads = []
    for head in range(GROUP):
        strip = strip_ref[head]
        heads.append(
            jnp.concatenate(
                [strip[:, WIN * (WIN - 1 - a) : WIN * (WIN - 1 - a) + HEAD] for a in range(WIN)], axis=0
            )
        )
    bias = jnp.concatenate(heads, axis=1)

    lane_head = lax.broadcasted_iota(jnp.int32, (WIN * WIN, WIDE), 1) // HEAD
    ones = (
        lax.broadcasted_iota(jnp.int32, (WIDE, WIDE), 0) // HEAD
        == lax.broadcasted_iota(jnp.int32, (WIDE, WIDE), 1) // HEAD
    ).astype(BF16)

    def spread(block):
        return jnp.concatenate(
            [jnp.where(lane_head == head, block, jnp.zeros_like(block)) for head in range(GROUP)], axis=0
        )

    plans = [(0, SHIFT, SHIFT, jnp.concatenate([prev_k, k[:SHIFT]], 0), jnp.concatenate([prev_v, v[:SHIFT]], 0))]
    for first in range(SHIFT, columns - SHIFT, WIN):
        plans.append((first, WIN, 0, k[first : first + WIN], v[first : first + WIN]))
    last = columns - SHIFT
    plans.append((last, SHIFT, 0, jnp.concatenate([k[last:], next_k], 0), jnp.concatenate([v[last:], next_v], 0)))

    for first, width, a_from, keys, values in plans:
        rows = width * WIN
        bias_rows = bias[a_from * WIN : a_from * WIN + rows]
        row_lat = lax.broadcasted_iota(jnp.int32, (rows, WIDE), 0) % WIN
        lane = lax.broadcasted_iota(jnp.int32, (rows, WIDE), 1)
        allowed = (row_lat < SHIFT) == (lane % WIN < SHIFT)
        own = lane // HEAD
        for w in range(lat_windows):
            span = slice(w * WIN, (w + 1) * WIN)
            qw = q[first : first + width, span].reshape(rows, WIDE).astype(BF16)
            kw = keys[:, span].reshape(WIN * WIN, WIDE).astype(BF16)
            vw = values[:, span].reshape(WIN * WIN, WIDE).astype(BF16)
            scores = lax.dot_general(qw, spread(kw), (((1,), (1,)), ((), ())), preferred_element_type=F32)
            scores = scores + bias_rows
            if w == lat_windows - 1:
                scores = jnp.where(allowed, scores, -1000000000.0)
            highest = jnp.zeros_like(scores)
            for head in range(GROUP):
                top = jnp.max(scores[:, head * HEAD : (head + 1) * HEAD], axis=-1, keepdims=True)
                highest = jnp.where(own == head, top, highest)
            weights = jnp.exp(scores - highest).astype(BF16)
            mixed = jnp.dot(weights, spread(vw), preferred_element_type=F32)
            sums = jnp.dot(weights, ones, preferred_element_type=F32)
            rolled[first : first + width, span] = (mixed / sums).reshape(width, WIN, WIDE)

    back = rolled[...]
    attended = jnp.concatenate([back[:, lats - SHIFT :], back[:, : lats - SHIFT]], axis=1)
    attended = attended.reshape(columns * lats, WIDE).astype(BF16)
    part = jnp.dot(attended, weight_ref[...], preferred_element_type=F32)

    @pl.when(step == 0)
    def _():
        total[...] = part

    @pl.when(step > 0)
    def _():
        total[...] += part

    @pl.when(step == pl.num_programs(0) - 1)
    def _():
        resid = (tokens_ref[...].astype(F32) + total[...]).astype(BF16)
        resid_ref[...] = resid
        resid_f = resid.astype(F32)
        scale = lax.rsqrt(jnp.mean(resid_f * resid_f, axis=-1, keepdims=True) + 1e-05)
        normed = (resid_f * scale * gain_ref[...]).astype(BF16)
        normed_ref[...] = normed
        logits = jnp.dot(normed, router_ref[...], preferred_element_type=F32)
        expert = lax.broadcasted_iota(jnp.int32, logits.shape, 1)
        picked = jnp.sum(jnp.where(chosen_ref[...] == expert, logits, 0.0), axis=-1, keepdims=True)
        gate_ref[...] = jax.nn.sigmoid(picked)


def front(tokens, qkv, from_prev, from_next, strips, out_weight, norm_gain, router, chosen):
    _, columns, lats, features = qkv.shape
    count = columns * lats
    experts = router.shape[1]
    slab = lambda which: pl.BlockSpec((1, columns, lats, WIDE), lambda g: (which, 0, 0, g))
    rim = pl.BlockSpec((2, SHIFT, lats, WIDE), lambda g: (0, 0, 0, g))
    whole = lambda *shape: pl.BlockSpec(shape, lambda g: (0,) * len(shape))
    return pl.pallas_call(
        front_kernel,
        grid=(features // WIDE,),
        in_specs=[
            slab(0), slab(1), slab(2), rim, rim,
            pl.BlockSpec((GROUP, WIN, 128), lambda g: (g, 0, 0)),
            pl.BlockSpec((WIDE, features), lambda g: (g, 0)),
            whole(count, features), whole(1, features), whole(features, experts), whole(count, 1),
        ],
        out_specs=[whole(count, features), whole(count, features), whole(count, 1)],
        out_shape=[
            jax.ShapeDtypeStruct((count, features), BF16),
            jax.ShapeDtypeStruct((count, features), BF16),
            jax.ShapeDtypeStruct((count, 1), F32),
        ],
        scratch_shapes=[pltpu.VMEM((count, features), F32), pltpu.VMEM((columns, lats, WIDE), F32)],
        compiler_params=pltpu.CompilerParams(vmem_limit_bytes=56 * 1024 * 1024),
        name="front",
    )(
        qkv, qkv, qkv, from_prev, from_next, strips, out_weight, tokens.reshape(count, features),
        norm_gain[None, :], router, chosen,
    )


def expert_apply(rows_in, up_local, down_local):
    features = rows_in.shape[-1]
    flat_rows = rows_in.reshape(-1, features)
    hidden = jax.nn.gelu(jnp.dot(flat_rows, up_local, preferred_element_type=F32)).astype(BF16)
    result = jnp.dot(hidden, down_local, preferred_element_type=F32).astype(BF16)
    return result.reshape(rows_in.shape)


def local(
    tokens,
    qkv,
    bias_table,
    out_weight,
    norm_gain,
    router,
    expert_ids,
    slot_expert,
    up_weight,
    down_weight,
):
    columns, lat_count, features = tokens.shape
    token_count = columns * lat_count
    from_next = from_behind(qkv[1:, :SHIFT], "lon", -1)
    from_prev = from_behind(qkv[1:, columns - SHIFT :], "lon", 1)
    strips = jnp.dot(bias_table, bias_spread(), precision=lax.Precision.HIGHEST).reshape(-1, WIN, 128)
    resid, normed, gate = front(
        tokens, qkv, from_prev, from_next, strips, out_weight, norm_gain, router,
        expert_ids.reshape(token_count, 1),
    )
    peers = lax.axis_size("lon")
    experts = up_weight.shape[0] * peers
    capacity = 2 * token_count // experts
    chosen = expert_ids.reshape(-1)
    expert_range = jnp.arange(experts, dtype=jnp.int32)
    chosen_hot = chosen[:, None] == expert_range[None, :]
    slot_of = jnp.sum(
        jnp.where(slot_expert[None, :] == expert_range[:, None], expert_range[None, :], 0), axis=1
    )
    target = jnp.sum(jnp.where(chosen_hot, slot_of[None, :], 0), axis=1)
    target_hot = (target[:, None] == jnp.arange(peers, dtype=jnp.int32)[None, :]).astype(jnp.int32)
    earlier = jnp.cumsum(target_hot, axis=0) - target_hot
    position = target * capacity + jnp.sum(earlier * target_hot, axis=1)
    selector = (position[None, :] == jnp.arange(peers * capacity, dtype=jnp.int32)[:, None]).astype(BF16)
    outgoing = jnp.dot(selector, normed, preferred_element_type=F32).astype(BF16)
    outgoing = outgoing.reshape(peers, capacity, features)
    incoming = lax.all_to_all(outgoing, "lon", split_axis=0, concat_axis=0, tiled=True)
    answers = expert_apply(incoming, up_weight[0], down_weight[0])
    returned = lax.all_to_all(answers, "lon", split_axis=0, concat_axis=0, tiled=True)
    gathered = jnp.einsum(
        "st,sd->td", selector, returned.reshape(-1, features), preferred_element_type=F32
    )
    blended = resid.astype(F32) + gate * gathered
    return blended.astype(BF16).reshape(columns, lat_count, features)


def solution(mesh):
    in_specs = (
        P(("groups", "lon"), None, None),
        P(None, ("groups", "lon"), None, None),
        P(),
        P(),
        P(),
        P(),
        P(("groups", "lon"), None, None),
        P(),
        P("lon", None, None),
        P("lon", None, None),
    )
    out_specs = P(("groups", "lon"), None, None)
    return jax.shard_map(local, mesh=mesh, in_specs=in_specs, out_specs=out_specs, check_vma=False)
```

time: 273 us -> 214 us (0.78)
  local copies, waits for them, and re-layouts: 63.2 us -> 6.74 us
  Pallas kernels: 0 us -> 17.9 us
  matrix products: 33 us -> 19.7 us
  other arithmetic: 12.9 us -> 3.79 us
  waiting for transfers between devices: 70.1 us -> 78.6 us
  blocking collectives: 82.4 us -> 77.1 us
    another operation x8 -> x1, local copies, waits for them, and re-layouts: 22.1 us -> 0.01 us  [the longest x3 6.73 us: to_windows(): grid.reshape(lon_count // WIN, WIN, lat_count // WIN, WIN, features)]
    pallas_call x0 -> x1, Pallas kernels: none -> 17.9 us  [front(): pl.pallas_call(front_kernel, grid=(features // WIDE,), in_specs=[slab(0),...]
    gather x2 -> x0, local copies, waits for them, and re-layouts: 17.8 us -> none  [attend(): scores = scores + bias_table[:, bias_index()][None]]
    dot_general x6 -> x3, matrix products: 27.6 us -> 15.8 us  [the longest x1 10.8 us: expert_apply(): jnp.dot(hidden, down_local, preferred_element_type=F32).astype(BF16)]
    convert_element_type x2 -> x0, local copies, waits for them, and re-layouts: 10.2 us -> none  [attend(): attended.reshape(win_count, WIN * WIN, head_count * HEAD)]
    concatenate x4 -> x0, other arithmetic: 8.39 us -> none  [the longest x2 3.77 us: local(): rolled = jnp.roll(qkv, -SHIFT, axis=2)]
    ppermute x2, waiting for transfers between devices: 3.19 us -> 9.79 us  [from_behind(): return lax.ppermute(value, axis, pairs)]
    slice x4 -> x2, local copies, waits for them, and re-layouts: 9.53 us -> 3.02 us  [the longest x1 2.8 us: local(): from_next = from_behind(qkv[1:, :SHIFT], 'lon', -1)]
  transfers between devices with their start and end apart: 3 -> 3, of which waited for: 2 -> 3; matrix products, arithmetic and copies ran while one was open for 10% -> 4% of each run, Pallas kernels for 0% -> 0%
where the time goes in v1:
time: 214 us; the launch traced here: 210 us
  waiting for transfers between devices  78.6 us (37%)
  blocking collectives  77.1 us (36%)
  matrix products  19.7 us (9%)
  Pallas kernels  17.9 us (8%)
  local copies, waits for them, and re-layouts  6.74 us (3%)
  starting transfers between devices  6.46 us (3%)
  other arithmetic  3.79 us (2%)
    all_to_all x1, blocking collectives, local(): lax.all_to_all(outgoing, 'lon', split_axis=0, concat_axis=0, tiled=True)  77.1 us
    all_to_all x1, waiting for transfers between devices, local(): lax.all_to_all(answers, 'lon', split_axis=0, concat_axis=0, tiled=True)  68.8 us
    pallas_call x1, Pallas kernels, front(): pl.pallas_call(front_kernel, grid=(features // WIDE,), in_specs=[slab(0),...  17.9 us
    dot_general x1, matrix products, expert_apply(): jnp.dot(hidden, down_local, preferred_element_type=F32).astype(BF16)  10.8 us
    ppermute x2, waiting for transfers between devices, from_behind(): return lax.ppermute(value, axis, pairs)  9.79 us
    all_to_all x1, starting transfers between devices, local(): lax.all_to_all(answers, 'lon', split_axis=0, concat_axis=0, tiled=True)  4.69 us
  transfers between devices with their start and end apart: 3, of which 3 were waited for; matrix products, arithmetic and copies ran while one was open for 4% of the time, Pallas kernels for 0%

profile of v1, /device:TPU:9, one launch (start us, length us, event | category | flops | bytes accessed | tf_op | source)
XLA Modules:
  0.0 210.4 jit_solution(4008372777141787640)
XLA Ops:
  0.0 0.0 copy-start
  0.0 0.0 copy-start.6
  0.0 0.0 copy-start.5
  0.0 2.8 %fusion.31 = (bf16[2,4,32,1536]{3,2,1,0:T(8,128)(2,1)}, bf16[2,4,32,1536]{3,2,1,0:T(8,128)(2,1)}) fusion(bf16[3,16,32,1536]{3,2,1,0:T(8,128)(2,1)} %v_ref.1), kind=kLoop, calls=%fused_computation.42 | loop fusion | bytes 3145728 | tf_op jit(solution)/shard_map/slice | solution.py:187
  2.8 0.7 collective-permute-start.1
  3.5 1.1 collective-permute-start
  4.6 0.1 select_reduce_fusion.1
  4.7 0.1 eq.64
  4.8 0.0 copy-done.6
  4.8 0.6 broadcast_in_dim.36.gain_ref
  5.4 0.5 broadcast.28
  5.9 0.6 reduce.8
  6.5 0.1 select_reduce_fusion
  6.6 1.2 reduce-window.6
  7.7 0.2 slice_reduce_fusion
  8.0 1.9 convolution_bitcast_fusion
  9.9 0.7 copy.20
  10.5 0.9 reshape.58.chosen_ref
  11.5 0.0 copy-done.3
  11.5 0.9 copy.16.router_ref
  12.4 0.1 fusion.25
  12.5 8.7 %collective-permute-done.1.next_ref = bf16[2,4,32,1536]{3,2,1,0:T(8,128)(2,1)} collective-permute-done((bf16[2,4,32,1536]{3,2,1,0:T(8,128)(2,1)}, bf16[2,4,32,1536]{3,2,1,0:T(8,128)(2,1)}, u32[]{:S(2)}, u32[]{:S(2)}) %collective-permute-start.1) | collective-permute-done | bytes 786464 | tf_op jit(solution)/shard_map/ppermute | solution.py:23
  21.2 1.1 collective-permute-done.prev_ref
  22.3 17.9 %front.1 = (bf16[512,1536]{1,0:T(8,128)(2,1)}, bf16[512,1536]{1,0:T(8,128)(2,1)}, f32[512,1]{1,0:T(8,128)}) custom-call(bf16[3,16,32,1536]{3,2,1,0:T(8,128)(2,1)} %v_ref.1, bf16[3,16,32,1536]{3,2,1,0:T(8,128)(2,1)} %v_ref.1, bf16[3,16,32,1536]{3,2,1,0:T(8,128)(2,1)} %v_ref.1, bf16[2,4,32,1536]{3,2,1,0:T(8,128)(2,1)} %collective-permute-done.prev_ref, ...), custom_call_target="tpu_custom_call" | custom-call | tf_op jit(solution)/shard_map/front/pallas_call | solution.py:141
  40.2 3.2 %convolution_convert_fusion = bf16[1024,1536]{1,0:T(8,128)(2,1)S(1)} fusion(bf16[512,1536]{1,0:T(8,128)(2,1)} %get-tuple-element.10, s32[512]{0:T(512)S(1)} %multiply_add_fusion), kind=kOutput, calls=%fused_computation.9 | convolution fusion | flops 1612709888 | bytes 4720640 | tf_op jit(solution)/shard_map/dot_general | solution.py:208
  43.4 77.1 %all_to_all.10 = bf16[32,32,1536]{2,1,0:T(8,128)(2,1)} all-to-all(bf16[32,32,1536]{2,1,0:T(8,128)(2,1)S(1)} %bitcast.48), channel_id=1, replica_groups=mesh['groups'=1,'lon'=32] {'lon'}, dimensions={0} | all-to-all | bytes 6291456 | tf_op jit(solution)/shard_map/all_to_all | solution.py:210
  120.5 10.8 %convolution_convert_fusion.1 = bf16[1024,1536]{1,0:T(8,128)(2,1)} fusion(bf16[1,1024,1536]{2,1,0:T(8,128)(2,1)S(1)} %copy-done, bf16[1024,1536]{1,0:T(8,128)(2,1)} %bitcast.49, bf16[1,1536,1024]{2,1,0:T(8,128)(2,1)} %param.19), kind=kOutput, calls=%fused_computation.10 | convolution fusion | flops 6453460992 | bytes 12582912 | tf_op jit(solution)/shard_map/dot_general | solution.py:169
  131.3 4.7 %all-to-all-start.1 = ((bf16[32,32,1536]{2,1,0:T(8,128)(2,1)}), bf16[32,32,1536]{2,1,0:T(8,128)(2,1)}, u32[]{:S(2)}, u32[]{:S(2)}) async-start(bf16[32,32,1536]{2,1,0:T(8,128)(2,1)} %bitcast.47), calls=%async_computation.1 | async-start | bytes 6291456 | tf_op jit(solution)/shard_map/all_to_all | solution.py:212
  136.0 0.1 reduce.1
  136.2 68.8 %all-to-all-done.1 = bf16[32,32,1536]{2,1,0:T(8,128)(2,1)} async-done(((bf16[32,32,1536]{2,1,0:T(8,128)(2,1)}), bf16[32,32,1536]{2,1,0:T(8,128)(2,1)}, u32[]{:S(2)}, u32[]{:S(2)}) %all-to-all-start.1) | async-done | bytes 3145760 | tf_op jit(solution)/shard_map/all_to_all | solution.py:212
  205.0 3.9 %fusion.16 = f32[512,1536]{1,0:T(8,128)S(1)} fusion(bf16[1024,1536]{1,0:T(8,128)(2,1)} %bitcast.9, s32[512]{0:T(512)S(1)} %multiply_add_fusion), kind=kOutput, calls=%fused_computation.20 | convolution fusion | flops 1611137024 | bytes 6293504 | tf_op jit(solution)/shard_map/st,sd->td/dot_general | solution.py:213
  208.9 1.6 add_convert_fusion
  (15 shorter events, 0.1 us)
Async XLA Ops:
  0.0 120.5 %copy-start = (bf16[1,1024,1536]{2,1,0:T(8,128)(2,1)S(1)}, bf16[1,1024,1536]{2,1,0:T(8,128)(2,1)}, u32[]{:S(2)}) copy-start(bf16[1,1024,1536]{2,1,0:T(8,128)(2,1)} %param.20) | copy-start | bytes 9437188
  0.0 4.6 %copy-start.7 = (s32[32]{0:T(128)S(1)}, s32[32]{0:T(128)}, u32[]{:S(2)}) copy-start(s32[32]{0:T(128)} %param.18) | copy-start | bytes 388
  0.0 4.7 %copy-start.4 = (s32[16,32,1]{1,2,0:T(1,128)S(1)}, s32[16,32,1]{1,2,0:T(1,128)}, u32[]{:S(2)}) copy-start(s32[16,32,1]{1,2,0:T(1,128)} %param.17) | copy-start | bytes 6148
  0.0 4.8 %copy-start.6 = (f32[1536]{0:T(1024)S(1)}, f32[1536]{0:T(1024)}, u32[]{:S(2)}) copy-start(f32[1536]{0:T(1024)} %param.15) | copy-start | bytes 18436
  0.0 8.0 %copy-start.5 = (f32[24,225]{1,0:T(8,128)S(1)}, f32[24,225]{1,0:T(8,128)}, u32[]{:S(2)}) copy-start(f32[24,225]{1,0:T(8,128)} %param.13) | copy-start | bytes 64804
  0.0 11.5 %copy-start.3 = (bf16[1536,32]{0,1:T(8,128)(2,1)S(1)}, bf16[1536,32]{0,1:T(8,128)(2,1)}, u32[]{:S(2)}) copy-start(bf16[1536,32]{0,1:T(8,128)(2,1)} %param.16) | copy-start | bytes 294916
  2.8 18.3 %collective-permute-start.1 = (bf16[2,4,32,1536]{3,2,1,0:T(8,128)(2,1)}, bf16[2,4,32,1536]{3,2,1,0:T(8,128)(2,1)}, u32[]{:S(2)}, u32[]{:S(2)}) collective-permute-start(bf16[2,4,32,1536]{3,2,1,0:T(8,128)(2,1)} %get-tuple-element.11), channel_id=1, source_target_pairs={{0,31},{1,0},{2,1},{3,2},{4,3},{5,4},{6,5},{7,6},{8,7},{9,8},{10,9... | collective-permute-start | bytes 2359304 | tf_op jit(solution)/shard_map/ppermute | solution.py:23
  3.5 18.8 %collective-permute-start = (bf16[2,4,32,1536]{3,2,1,0:T(8,128)(2,1)}, bf16[2,4,32,1536]{3,2,1,0:T(8,128)(2,1)}, u32[]{:S(2)}, u32[]{:S(2)}) collective-permute-start(bf16[2,4,32,1536]{3,2,1,0:T(8,128)(2,1)} %get-tuple-element.12), channel_id=1, source_target_pairs={{0,1},{1,2},{2,3},{3,4},{4,5},{5,6},{6,7},{7,8},{8,9},{9,10},{10,1... | collective-permute-start | bytes 2359304 | tf_op jit(solution)/shard_map/ppermute | solution.py:23
  131.3 4.7 %copy-start.2 = (f32[512,1]{1,0:T(8,128)S(1)}, f32[512,1]{1,0:T(8,128)}, u32[]{:S(2)}) copy-start(f32[512,1]{1,0:T(8,128)} %get-tuple-element.9) | copy-start | bytes 6148
  131.3 73.7 %all-to-all-start.1 = ((bf16[32,32,1536]{2,1,0:T(8,128)(2,1)}), bf16[32,32,1536]{2,1,0:T(8,128)(2,1)}, u32[]{:S(2)}, u32[]{:S(2)}) async-start(bf16[32,32,1536]{2,1,0:T(8,128)(2,1)} %bitcast.47), calls=%async_computation.1 | async-start | bytes 6291456 | tf_op jit(solution)/shard_map/all_to_all | solution.py:212
  205.0 3.9 %copy-start.1 = (bf16[512,1536]{1,0:T(8,128)(2,1)S(1)}, bf16[512,1536]{1,0:T(8,128)(2,1)}, u32[]{:S(2)}) copy-start(bf16[512,1536]{1,0:T(8,128)(2,1)} %get-tuple-element.8) | copy-start | bytes 4718596

commit v2 on v1

--- a/solution.py
+++ b/solution.py
@@ -13,6 +13,7 @@
 SHIFT = 4
 GROUP = 4
 WIDE = GROUP * HEAD
+QUARTERS = 4
 F32 = jnp.float32
 BF16 = jnp.bfloat16
 
@@ -162,12 +163,160 @@
     )
 
 
-def expert_apply(rows_in, up_local, down_local):
-    features = rows_in.shape[-1]
-    flat_rows = rows_in.reshape(-1, features)
-    hidden = jax.nn.gelu(jnp.dot(flat_rows, up_local, preferred_element_type=F32)).astype(BF16)
-    result = jnp.dot(hidden, down_local, preferred_element_type=F32).astype(BF16)
-    return result.reshape(rows_in.shape)
+def expert_kernel(
+    peers, place_row_ref, place_col_ref, normed_ref, resid_ref, gate_ref, up_hbm, down_hbm, out_ref,
+    outgoing, incoming, answers, returned, total, up, down, load_sem, send_sem, recv_sem, back_sem, home_sem,
+):
+    me = lax.axis_index("lon")
+    size = peers // QUARTERS
+    rows = outgoing.shape[0] // QUARTERS
+    cap = rows // size
+    count = normed_ref.shape[0]
+    mine, inner = me // size, me % size
+
+    def block(index):
+        return pl.ds(pl.multiple_of(index * cap, cap), cap)
+
+    def span(quarter):
+        return pl.ds(pl.multiple_of(quarter * rows, rows), rows)
+
+    def there(target):
+        return pltpu.make_async_remote_copy(
+            src_ref=outgoing.at[block(target)], dst_ref=incoming.at[block(me)],
+            send_sem=send_sem.at[target], recv_sem=recv_sem.at[me],
+            device_id={"lon": target}, device_id_type=pl.DeviceIdType.MESH,
+        )
+
+    def back(source):
+        return pltpu.make_async_remote_copy(
+            src_ref=answers.at[block(source)], dst_ref=returned.at[block(me)],
+            send_sem=back_sem.at[source], recv_sem=home_sem.at[me],
+            device_id={"lon": source}, device_id_type=pl.DeviceIdType.MESH,
+        )
+
+    def landed(buffer, sems, source):
+        return pltpu.make_async_remote_copy(
+            src_ref=buffer.at[block(source)], dst_ref=buffer.at[block(source)],
+            send_sem=sems.at[source], recv_sem=sems.at[source],
+            device_id={"lon": source}, device_id_type=pl.DeviceIdType.MESH,
+        )
+
+    barrier = pltpu.get_barrier_semaphore()
+
+    @pl.loop(1, peers)
+    def _(offset):
+        pl.semaphore_signal(
+            barrier, inc=1, device_id={"lon": lax.rem(me + offset, peers)}, device_id_type=pl.DeviceIdType.MESH
+        )
+
+    load_up = pltpu.make_async_copy(up_hbm.at[0], up, load_sem.at[0])
+    load_down = pltpu.make_async_copy(down_hbm.at[0], down, load_sem.at[1])
+    load_up.start()
+    load_down.start()
+    pl.semaphore_wait(barrier, peers - 1)
+
+    @pl.loop(0, QUARTERS)
+    def _(step):
+        quarter = lax.rem(mine + step + 2, QUARTERS)
+        slot = quarter * rows + lax.broadcasted_iota(jnp.int32, (rows, count), 0)
+        pick = jnp.where(slot == place_row_ref[...], 1.0, 0.0).astype(BF16)
+        outgoing[span(quarter), :] = jnp.dot(pick, normed_ref[...], preferred_element_type=F32).astype(BF16)
+
+        @pl.loop(0, size)
+        def _(offset):
+            target = quarter * size + lax.rem(inner + offset, size)
+
+            @pl.when(target != me)
+            def _():
+                there(target).start()
+
+            @pl.when(target == me)
+            def _():
+                incoming[block(me), :] = outgoing[block(me), :]
+
+    load_up.wait()
+    load_down.wait()
+
+    @pl.loop(0, QUARTERS)
+    def _(step):
+        quarter = lax.rem(mine + 2 * QUARTERS - step - 2, QUARTERS)
+
+        @pl.loop(0, size)
+        def _(offset):
+            source = quarter * size + offset
+
+            @pl.when(source != me)
+            def _():
+                landed(incoming, recv_sem, source).wait_recv()
+
+        inputs = incoming[span(quarter), :]
+        hidden = jax.nn.gelu(jnp.dot(inputs, up[...], preferred_element_type=F32)).astype(BF16)
+        answers[span(quarter), :] = jnp.dot(hidden, down[...], preferred_element_type=F32).astype(BF16)
+
+        @pl.loop(0, size)
+        def _(offset):
+            source = quarter * size + lax.rem(inner + size - offset, size)
+
+            @pl.when(source != me)
+            def _():
+                back(source).start()
+
+            @pl.when(source == me)
+            def _():
+                returned[block(me), :] = answers[block(me), :]
+
+    total[...] = jnp.zeros_like(total)
+
+    @pl.loop(0, QUARTERS)
+    def _(step):
+        quarter = lax.rem(mine + step + 2, QUARTERS)
+
+        @pl.loop(0, size)
+        def _(offset):
+            source = quarter * size + offset
+
+            @pl.when(source != me)
+            def _():
+                landed(returned, home_sem, source).wait_recv()
+
+        slot = quarter * rows + lax.broadcasted_iota(jnp.int32, (count, rows), 1)
+        pick = jnp.where(slot == place_col_ref[...], 1.0, 0.0).astype(BF16)
+        total[...] += jnp.dot(pick, returned[span(quarter), :], preferred_element_type=F32)
+
+    out_ref[...] = (resid_ref[...].astype(F32) + gate_ref[...] * total[...]).astype(BF16)
+
+    @pl.loop(0, peers)
+    def _(target):
+        @pl.when(target != me)
+        def _():
+            there(target).wait_send()
+            back(target).wait_send()
+
+
+def expert_layer(position, normed, resid, gate, up_weight, down_weight, slots):
+    count, features = normed.shape
+    hidden = up_weight.shape[-1]
+    peers = lax.axis_size("lon")
+    vmem = pl.BlockSpec(memory_space=pltpu.VMEM)
+    hbm = pl.BlockSpec(memory_space=pl.ANY)
+    return pl.pallas_call(
+        functools.partial(expert_kernel, peers),
+        out_shape=jax.ShapeDtypeStruct((count, features), BF16),
+        in_specs=[vmem] * 5 + [hbm] * 2,
+        out_specs=vmem,
+        scratch_shapes=[pltpu.VMEM((slots, features), BF16)] * 4
+        + [
+            pltpu.VMEM((count, features), F32),
+            pltpu.VMEM((features, hidden), BF16),
+            pltpu.VMEM((hidden, features), BF16),
+            pltpu.SemaphoreType.DMA((2,)),
+        ]
+        + [pltpu.SemaphoreType.DMA((peers,))] * 4,
+        compiler_params=pltpu.CompilerParams(
+            collective_id=1, has_side_effects=True, vmem_limit_bytes=56 * 1024 * 1024
+        ),
+        name="experts",
+    )(position[None, :], position[:, None], normed, resid, gate, up_weight, down_weight)
 
 
 def local(
@@ -204,17 +353,8 @@
     target_hot = (target[:, None] == jnp.arange(peers, dtype=jnp.int32)[None, :]).astype(jnp.int32)
     earlier = jnp.cumsum(target_hot, axis=0) - target_hot
     position = target * capacity + jnp.sum(earlier * target_hot, axis=1)
-    selector = (position[None, :] == jnp.arange(peers * capacity, dtype=jnp.int32)[:, None]).astype(BF16)
-    outgoing = jnp.dot(selector, normed, preferred_element_type=F32).astype(BF16)
-    outgoing = outgoing.reshape(peers, capacity, features)
-    incoming = lax.all_to_all(outgoing, "lon", split_axis=0, concat_axis=0, tiled=True)
-    answers = expert_apply(incoming, up_weight[0], down_weight[0])
-    returned = lax.all_to_all(answers, "lon", split_axis=0, concat_axis=0, tiled=True)
-    gathered = jnp.einsum(
-        "st,sd->td", selector, returned.reshape(-1, features), preferred_element_type=F32
-    )
-    blended = resid.astype(F32) + gate * gathered
-    return blended.astype(BF16).reshape(columns, lat_count, features)
+    blended = expert_layer(position, normed, resid, gate, up_weight, down_weight, peers * capacity)
+    return blended.reshape(columns, lat_count, features)
 
 
 def solution(mesh):

time: 214 us -> 195 us (0.911)
  Pallas kernels: 17.9 us -> 166 us
  blocking collectives: 77.1 us -> 0 us
  waiting for transfers between devices: 78.6 us -> 8.66 us
  matrix products: 19.7 us -> 0.67 us
  local copies, waits for them, and re-layouts: 6.74 us -> 11.8 us
  starting transfers between devices: 6.46 us -> 1.77 us
    pallas_call x0 -> x1, Pallas kernels: none -> 148 us  [expert_layer(): pl.pallas_call(functools.partial(expert_kernel, peers), out_shape=jax.Sha...]
    all_to_all x1 -> x0, blocking collectives: 77.1 us -> none  [local(): lax.all_to_all(outgoing, 'lon', split_axis=0, concat_axis=0, tiled=True)]
    all_to_all x1 -> x0, waiting for transfers between devices: 68.8 us -> none  [local(): lax.all_to_all(answers, 'lon', split_axis=0, concat_axis=0, tiled=True)]
    dot_general x3 -> x0, matrix products: 17.8 us -> none  [the longest x1 10.8 us: expert_apply(): jnp.dot(hidden, down_local, preferred_element_type=F32).astype(BF16)]
    all_to_all x1 -> x0, starting transfers between devices: 4.69 us -> none  [local(): lax.all_to_all(answers, 'lon', split_axis=0, concat_axis=0, tiled=True)]
    unnamed x19 -> x20, local copies, waits for them, and re-layouts: 2.09 us -> 6.65 us
  transfers between devices with their start and end apart: 3 -> 2, of which waited for: 3 -> 2; matrix products, arithmetic and copies ran while one was open for 4% -> 5% of each run, Pallas kernels for 0% -> 0%
where the time goes in v2:
time: 195 us; the launch traced here: 191 us
  Pallas kernels  166 us (85%)
  local copies, waits for them, and re-layouts  11.8 us (6%)
  waiting for transfers between devices  8.66 us (4%)
  other arithmetic  2.23 us (1%)
    pallas_call x1, Pallas kernels, expert_layer(): pl.pallas_call(functools.partial(expert_kernel, peers), out_shape=jax.Sha...  148 us
    pallas_call x1, Pallas kernels, front(): pl.pallas_call(front_kernel, grid=(features // WIDE,), in_specs=[slab(0),...  17.9 us
    ppermute x2, waiting for transfers between devices, from_behind(): return lax.ppermute(value, axis, pairs)  8.66 us
    unnamed x20, local copies, waits for them, and re-layouts  6.65 us
  transfers between devices with their start and end apart: 2, of which 2 were waited for; matrix products, arithmetic and copies ran while one was open for 5% of the time, Pallas kernels for 0%

profile of v2, /device:TPU:9, one launch (start us, length us, event | category | flops | bytes accessed | tf_op | source)
XLA Modules:
  0.0 191.4 jit_solution(11092913717659916267)
XLA Ops:
  0.0 0.0 copy-start
  0.0 0.0 copy-start.6
  0.0 0.0 copy-start.4
  0.0 2.5 %fusion.4 = (bf16[2,4,32,1536]{3,2,1,0:T(8,128)(2,1)}, bf16[2,4,32,1536]{3,2,1,0:T(8,128)(2,1)S(1)}) fusion(bf16[3,16,32,1536]{3,2,1,0:T(8,128)(2,1)} %v_ref.1), kind=kLoop, calls=%fused_computation.15 | loop fusion | bytes 3145728 | tf_op jit(solution)/shard_map/slice | solution.py:336
  2.5 0.7 collective-permute-start.1
  3.2 1.1 collective-permute-start
  4.3 0.0 copy-done.7
  4.3 0.1 select_reduce_fusion.1
  4.4 0.0 copy-done.6
  4.4 0.6 broadcast_in_dim.40.gain_ref
  5.0 0.6 broadcast.41
  5.6 0.0 copy-done.4
  5.6 0.7 reduce.7
  6.3 0.1 eq.51
  6.4 0.1 select_reduce_fusion
  6.5 1.2 reduce-window.6
  7.7 0.2 slice_reduce_fusion
  7.9 0.0 copy-done
  7.9 0.0 copy-done.1
  7.9 0.7 convolution_bitcast_fusion
  8.6 0.6 copy.22
  9.3 0.1 fusion.2
  9.4 0.8 copy.20.place_col_ref
  10.2 0.9 broadcast_in_dim_reshape.4.chosen_ref
  11.2 1.8 copy.18.router_ref
  13.0 8.0 %collective-permute-done.1.next_ref = bf16[2,4,32,1536]{3,2,1,0:T(8,128)(2,1)S(1)} collective-permute-done((bf16[2,4,32,1536]{3,2,1,0:T(8,128)(2,1)}, bf16[2,4,32,1536]{3,2,1,0:T(8,128)(2,1)S(1)}, u32[]{:S(2)}, u32[]{:S(2)}) %collective-permute-start.1) | collective-permute-done | bytes 786464 | tf_op jit(solution)/shard_map/ppermute | solution.py:24
  20.9 0.7 collective-permute-done.prev_ref
  21.6 0.2 copy-done.2
  21.8 0.7 copy-done.3
  22.5 17.9 %front.1 = (bf16[512,1536]{1,0:T(8,128)(2,1)}, bf16[512,1536]{1,0:T(8,128)(2,1)}, f32[512,1]{1,0:T(8,128)}) custom-call(bf16[3,16,32,1536]{3,2,1,0:T(8,128)(2,1)} %v_ref.1, bf16[3,16,32,1536]{3,2,1,0:T(8,128)(2,1)} %v_ref.1, bf16[3,16,32,1536]{3,2,1,0:T(8,128)(2,1)} %v_ref.1, bf16[2,4,32,1536]{3,2,1,0:T(8,128)(2,1)} %copy-done.3, ...), custom_call_target="tpu_custom_call" | custom-call | tf_op jit(solution)/shard_map/front/pallas_call | solution.py:142
  40.4 148.3 %experts.1 = bf16[512,1536]{1,0:T(8,128)(2,1)} custom-call(s32[1,512]{1,0:T(1,128)} %bitcast.38, s32[512,1]{1,0:T(8,128)} %copy.20.place_col_ref, bf16[512,1536]{1,0:T(8,128)(2,1)} %get-tuple-element.8.normed_ref, bf16[512,1536]{1,0:T(8,128)(2,1)} %get-tuple-element.9.resid_ref, f32[512,1]{1,0:T(8,128)} %get-tuple-element.10.gate_ref, ...), custom_call_target="tpu_custom_call" | custom-call | tf_op jit(solution)/shard_map/experts/pallas_call | solution.py:302
  188.7 2.7 %copy.25 = bf16[16,32,1536]{2,1,0:T(8,128)(2,1)} copy(bf16[16,32,1536]{2,1,0:T(8,128)(2,1)} %bitcast.32) | data formatting | bytes 3145728
  (10 shorter events, 0.1 us)
Async XLA Ops:
  0.0 7.9 %copy-start = (f32[24,225]{1,0:T(8,128)S(1)}, f32[24,225]{1,0:T(8,128)}, u32[]{:S(2)}) copy-start(f32[24,225]{1,0:T(8,128)} %param.13) | copy-start | bytes 64804
  0.0 7.9 %copy-start.1 = (f32[225,1024]{1,0:T(8,128)S(1)}, f32[225,1024]{1,0:T(8,128)}, u32[]{:S(2)}) copy-start(f32[225,1024]{1,0:T(8,128)} %constant.10.clone) | copy-start | bytes 2764804
  0.0 4.3 %copy-start.7 = (s32[32]{0:T(128)S(1)}, s32[32]{0:T(128)}, u32[]{:S(2)}) copy-start(s32[32]{0:T(128)} %param.18) | copy-start | bytes 388
  0.0 4.4 %copy-start.6 = (f32[1536]{0:T(1024)S(1)}, f32[1536]{0:T(1024)}, u32[]{:S(2)}) copy-start(f32[1536]{0:T(1024)} %param.15) | copy-start | bytes 18436
  0.0 5.6 %copy-start.4 = (s32[16,32,1]{1,2,0:T(1,128)S(1)}, s32[16,32,1]{1,2,0:T(1,128)}, u32[]{:S(2)}) copy-start(s32[16,32,1]{1,2,0:T(1,128)} %param.17) | copy-start | bytes 6148
  2.5 18.4 %collective-permute-start.1 = (bf16[2,4,32,1536]{3,2,1,0:T(8,128)(2,1)}, bf16[2,4,32,1536]{3,2,1,0:T(8,128)(2,1)S(1)}, u32[]{:S(2)}, u32[]{:S(2)}) collective-permute-start(bf16[2,4,32,1536]{3,2,1,0:T(8,128)(2,1)} %get-tuple-element.11), channel_id=1, source_target_pairs={{0,31},{1,0},{2,1},{3,2},{4,3},{5,4},{6,5},{7,6},{8,7},{9,8},{10,9... | collective-permute-start | bytes 2359304 | tf_op jit(solution)/shard_map/ppermute | solution.py:24
  3.2 18.5 %collective-permute-start = (bf16[2,4,32,1536]{3,2,1,0:T(8,128)(2,1)S(1)}, bf16[2,4,32,1536]{3,2,1,0:T(8,128)(2,1)S(1)}, u32[]{:S(2)}, u32[]{:S(2)}) collective-permute-start(bf16[2,4,32,1536]{3,2,1,0:T(8,128)(2,1)S(1)} %get-tuple-element.12), channel_id=1, source_target_pairs={{0,1},{1,2},{2,3},{3,4},{4,5},{5,6},{6,7},{7,8},{8,9},{9,10},{10,1... | collective-permute-start | bytes 2359304 | tf_op jit(solution)/shard_map/ppermute | solution.py:24
  9.4 31.0 %copy-start.5 = (s32[512]{0:T(512)}, s32[512]{0:T(512)S(1)}, u32[]{:S(2)}) copy-start(s32[512]{0:T(512)S(1)} %multiply_add_fusion) | copy-start | bytes 6148
  20.9 0.9 copy-start.2
  21.6 0.9 copy-start.3

commit v3 on v2

--- a/solution.py
+++ b/solution.py
@@ -16,12 +16,6 @@
 QUARTERS = 4
 F32 = jnp.float32
 BF16 = jnp.bfloat16
-
-
-def from_behind(value, axis, steps):
-    count = lax.axis_size(axis)
-    pairs = [(source, (source + steps) % count) for source in range(count)]
-    return lax.ppermute(value, axis, pairs)
 
 
 def bias_spread():
@@ -41,17 +35,49 @@
 
 
 def front_kernel(
-    q_ref, k_ref, v_ref, prev_ref, next_ref, strip_ref, weight_ref, tokens_ref, gain_ref,
-    router_ref, chosen_ref, resid_ref, normed_ref, gate_ref, total, rolled,
+    qkv_hbm, q_ref, k_ref, v_ref, strip_ref, weight_ref, tokens_ref, gain_ref, router_ref, chosen_ref,
+    slot_ref, resid_ref, normed_ref, gate_ref, place_col_ref, place_row_ref,
+    prev_ref, next_ref, total, rolled, prev_send, prev_recv, next_send, next_recv,
 ):
     step = pl.program_id(0)
     columns, lats = q_ref.shape[1], q_ref.shape[2]
+    groups = prev_ref.shape[0]
+    group = lax.rem(step, groups)
     lat_windows = lats // WIN
-    q = shift_up(q_ref[0]) * (1.0 / 8.0)
-    k = shift_up(k_ref[0])
-    v = shift_up(v_ref[0])
-    prev_k, prev_v = shift_up(prev_ref[0]), shift_up(prev_ref[1])
-    next_k, next_v = shift_up(next_ref[0]), shift_up(next_ref[1])
+    last = columns - SHIFT
+    rim = SHIFT * lats
+    me, peers = lax.axis_index("lon"), lax.axis_size("lon")
+    right, left = lax.rem(me + 1, peers), lax.rem(me + peers - 1, peers)
+
+    def up(index):
+        return pltpu.make_async_remote_copy(
+            src_ref=qkv_hbm.at[pl.ds(1, 2), pl.ds(last, SHIFT), :, pl.ds(pl.multiple_of(index * WIDE, WIDE), WIDE)],
+            dst_ref=prev_ref.at[index], send_sem=prev_send.at[index], recv_sem=prev_recv.at[index],
+            device_id={"lon": right}, device_id_type=pl.DeviceIdType.MESH,
+        )
+
+    def down(index):
+        return pltpu.make_async_remote_copy(
+            src_ref=qkv_hbm.at[pl.ds(1, 2), pl.ds(0, SHIFT), :, pl.ds(pl.multiple_of(index * WIDE, WIDE), WIDE)],
+            dst_ref=next_ref.at[index], send_sem=next_send.at[index], recv_sem=next_recv.at[index],
+            device_id={"lon": left}, device_id_type=pl.DeviceIdType.MESH,
+        )
+
+    @pl.when(step == 0)
+    def _():
+        barrier = pltpu.get_barrier_semaphore()
+        for neighbour in (left, right):
+            pl.semaphore_signal(
+                barrier, inc=1, device_id={"lon": neighbour}, device_id_type=pl.DeviceIdType.MESH
+            )
+        pl.semaphore_wait(barrier, 2)
+
+        @pl.loop(0, groups)
+        def _(index):
+            up(index).start()
+            down(index).start()
+
+        total[...] = tokens_ref[...].astype(F32)
 
     heads = []
     for head in range(GROUP):
@@ -64,9 +90,11 @@
     bias = jnp.concatenate(heads, axis=1)
 
     lane_head = lax.broadcasted_iota(jnp.int32, (WIN * WIN, WIDE), 1) // HEAD
-    ones = (
+    ones = jnp.where(
         lax.broadcasted_iota(jnp.int32, (WIDE, WIDE), 0) // HEAD
-        == lax.broadcasted_iota(jnp.int32, (WIDE, WIDE), 1) // HEAD
+        == lax.broadcasted_iota(jnp.int32, (WIDE, WIDE), 1) // HEAD,
+        1.0,
+        0.0,
     ).astype(BF16)
 
     def spread(block):
@@ -74,14 +102,9 @@
             [jnp.where(lane_head == head, block, jnp.zeros_like(block)) for head in range(GROUP)], axis=0
         )
 
-    plans = [(0, SHIFT, SHIFT, jnp.concatenate([prev_k, k[:SHIFT]], 0), jnp.concatenate([prev_v, v[:SHIFT]], 0))]
-    for first in range(SHIFT, columns - SHIFT, WIN):
-        plans.append((first, WIN, 0, k[first : first + WIN], v[first : first + WIN]))
-    last = columns - SHIFT
-    plans.append((last, SHIFT, 0, jnp.concatenate([k[last:], next_k], 0), jnp.concatenate([v[last:], next_v], 0)))
-
-    for first, width, a_from, keys, values in plans:
+    def attend(first, width, a_from, keys, values):
         rows = width * WIN
+        queries = shift_up(q_ref[0, first : first + width]) * (1.0 / 8.0)
         bias_rows = bias[a_from * WIN : a_from * WIN + rows]
         row_lat = lax.broadcasted_iota(jnp.int32, (rows, WIDE), 0) % WIN
         lane = lax.broadcasted_iota(jnp.int32, (rows, WIDE), 1)
@@ -89,7 +112,7 @@
         own = lane // HEAD
         for w in range(lat_windows):
             span = slice(w * WIN, (w + 1) * WIN)
-            qw = q[first : first + width, span].reshape(rows, WIDE).astype(BF16)
+            qw = queries[:, span].reshape(rows, WIDE).astype(BF16)
             kw = keys[:, span].reshape(WIN * WIN, WIDE).astype(BF16)
             vw = values[:, span].reshape(WIN * WIN, WIDE).astype(BF16)
             scores = lax.dot_general(qw, spread(kw), (((1,), (1,)), ((), ())), preferred_element_type=F32)
@@ -105,66 +128,113 @@
             sums = jnp.dot(weights, ones, preferred_element_type=F32)
             rolled[first : first + width, span] = (mixed / sums).reshape(width, WIN, WIDE)
 
-    back = rolled[...]
-    attended = jnp.concatenate([back[:, lats - SHIFT :], back[:, : lats - SHIFT]], axis=1)
-    attended = attended.reshape(columns * lats, WIDE).astype(BF16)
-    part = jnp.dot(attended, weight_ref[...], preferred_element_type=F32)
-
-    @pl.when(step == 0)
+    def project(back):
+        attended = jnp.concatenate([back[:, lats - SHIFT :], back[:, : lats - SHIFT]], axis=1)
+        attended = attended.reshape(-1, WIDE).astype(BF16)
+        return jnp.dot(attended, weight_ref[...], preferred_element_type=F32)
+
+    @pl.when(step < groups)
     def _():
-        total[...] = part
-
-    @pl.when(step > 0)
+        for first in range(SHIFT, last, WIN):
+            span = slice(first, first + WIN)
+            attend(first, WIN, 0, shift_up(k_ref[0, span]), shift_up(v_ref[0, span]))
+        total[rim : last * lats] += project(rolled[SHIFT:last])
+
+    @pl.when(step >= groups)
     def _():
-        total[...] += part
+        up(group).wait_recv()
+        down(group).wait_recv()
+        pairs = [
+            (0, SHIFT, lambda which, ref: jnp.concatenate([prev_ref[group, which], ref[0, :SHIFT]], 0)),
+            (last, 0, lambda which, ref: jnp.concatenate([ref[0, last:], next_ref[group, which]], 0)),
+        ]
+        for first, a_from, joined in pairs:
+            attend(first, SHIFT, a_from, shift_up(joined(0, k_ref)), shift_up(joined(1, v_ref)))
+        part = project(jnp.concatenate([rolled[:SHIFT], rolled[last:]], 0))
+        total[:rim] += part[:rim]
+        total[last * lats :] += part[rim:]
+
+    @pl.when(step == 1)
+    def _():
+        count, experts = chosen_ref.shape[0], slot_ref.shape[1]
+        cap = 2 * count // experts
+        hot = jnp.where(chosen_ref[...] == slot_ref[...], 1.0, 0.0)
+        row = lax.broadcasted_iota(jnp.int32, (count, count), 0)
+        col = lax.broadcasted_iota(jnp.int32, (count, count), 1)
+        before = jnp.where(col < row, 1.0, 0.0).astype(BF16)
+        earlier = jnp.dot(before, hot.astype(BF16), preferred_element_type=F32)
+        base = (lax.broadcasted_iota(jnp.int32, hot.shape, 1) * cap).astype(F32)
+        place = jnp.sum(hot * (base + earlier), axis=-1, keepdims=True)
+        place_col_ref[...] = place.astype(jnp.int32)
+        place_row_ref[...] = jnp.sum(jnp.where(row == col, place, 0.0), axis=0, keepdims=True).astype(jnp.int32)
 
     @pl.when(step == pl.num_programs(0) - 1)
     def _():
-        resid = (tokens_ref[...].astype(F32) + total[...]).astype(BF16)
+        resid = total[...].astype(BF16)
         resid_ref[...] = resid
         resid_f = resid.astype(F32)
         scale = lax.rsqrt(jnp.mean(resid_f * resid_f, axis=-1, keepdims=True) + 1e-05)
         normed = (resid_f * scale * gain_ref[...]).astype(BF16)
         normed_ref[...] = normed
-        logits = jnp.dot(normed, router_ref[...], preferred_element_type=F32)
+        logits = lax.dot_general(normed, router_ref[...], (((1,), (1,)), ((), ())), preferred_element_type=F32)
         expert = lax.broadcasted_iota(jnp.int32, logits.shape, 1)
         picked = jnp.sum(jnp.where(chosen_ref[...] == expert, logits, 0.0), axis=-1, keepdims=True)
         gate_ref[...] = jax.nn.sigmoid(picked)
 
-
-def front(tokens, qkv, from_prev, from_next, strips, out_weight, norm_gain, router, chosen):
+        @pl.loop(0, groups)
+        def _(index):
+            up(index).wait_send()
+            down(index).wait_send()
+
+
+def front(tokens, qkv, strips, out_weight, norm_gain, router, chosen, slot_expert):
     _, columns, lats, features = qkv.shape
     count = columns * lats
     experts = router.shape[1]
-    slab = lambda which: pl.BlockSpec((1, columns, lats, WIDE), lambda g: (which, 0, 0, g))
-    rim = pl.BlockSpec((2, SHIFT, lats, WIDE), lambda g: (0, 0, 0, g))
+    groups = features // WIDE
+    slab = lambda which: pl.BlockSpec((1, columns, lats, WIDE), lambda g: (which, 0, 0, g % groups))
     whole = lambda *shape: pl.BlockSpec(shape, lambda g: (0,) * len(shape))
+    halo = pltpu.VMEM((groups, 2, SHIFT, lats, WIDE), BF16)
     return pl.pallas_call(
         front_kernel,
-        grid=(features // WIDE,),
+        grid=(2 * groups,),
         in_specs=[
-            slab(0), slab(1), slab(2), rim, rim,
-            pl.BlockSpec((GROUP, WIN, 128), lambda g: (g, 0, 0)),
-            pl.BlockSpec((WIDE, features), lambda g: (g, 0)),
-            whole(count, features), whole(1, features), whole(features, experts), whole(count, 1),
+            pl.BlockSpec(memory_space=pl.ANY), slab(0), slab(1), slab(2),
+            pl.BlockSpec((GROUP, WIN, 128), lambda g: (g % groups, 0, 0)),
+            pl.BlockSpec((WIDE, features), lambda g: (g % groups, 0)),
+            whole(count, features), whole(1, features), whole(experts, features), whole(count, 1),
+            whole(1, experts),
         ],
-        out_specs=[whole(count, features), whole(count, features), whole(count, 1)],
+        out_specs=[
+            whole(count, features), whole(count, features), whole(count, 1), whole(count, 1), whole(1, count),
+        ],
         out_shape=[
             jax.ShapeDtypeStruct((count, features), BF16),
             jax.ShapeDtypeStruct((count, features), BF16),
             jax.ShapeDtypeStruct((count, 1), F32),
+            jax.ShapeDtypeStruct((count, 1), jnp.int32),
+            jax.ShapeDtypeStruct((1, count), jnp.int32),
         ],
-        scratch_shapes=[pltpu.VMEM((count, features), F32), pltpu.VMEM((columns, lats, WIDE), F32)],
-        compiler_params=pltpu.CompilerParams(vmem_limit_bytes=56 * 1024 * 1024),
+        scratch_shapes=[
+            halo, halo, pltpu.VMEM((count, features), F32), pltpu.VMEM((columns, lats, WIDE), F32),
+        ]
+        + [pltpu.SemaphoreType.DMA((groups,))] * 4,
+        compiler_params=pltpu.CompilerParams(
+            collective_id=0, has_side_effects=True, vmem_limit_bytes=56 * 1024 * 1024
+        ),
         name="front",
     )(
-        qkv, qkv, qkv, from_prev, from_next, strips, out_weight, tokens.reshape(count, features),
-        norm_gain[None, :], router, chosen,
+        qkv, qkv, qkv, qkv, strips, out_weight, tokens.reshape(count, features),
+        norm_gain[None, :], router.T, chosen, slot_expert[None, :],
     )
 
 
+def ahead(step):
+    return 2 + step - (step // 2) * (2 * step - 1)
+
+
 def expert_kernel(
-    peers, place_row_ref, place_col_ref, normed_ref, resid_ref, gate_ref, up_hbm, down_hbm, out_ref,
+    peers, place_row_ref, place_col_ref, normed_ref, up_hbm, down_hbm, out_ref,
     outgoing, incoming, answers, returned, total, up, down, load_sem, send_sem, recv_sem, back_sem, home_sem,
 ):
     me = lax.axis_index("lon")
@@ -217,7 +287,7 @@
 
     @pl.loop(0, QUARTERS)
     def _(step):
-        quarter = lax.rem(mine + step + 2, QUARTERS)
+        quarter = lax.rem(mine + ahead(step), QUARTERS)
         slot = quarter * rows + lax.broadcasted_iota(jnp.int32, (rows, count), 0)
         pick = jnp.where(slot == place_row_ref[...], 1.0, 0.0).astype(BF16)
         outgoing[span(quarter), :] = jnp.dot(pick, normed_ref[...], preferred_element_type=F32).astype(BF16)
@@ -239,7 +309,7 @@
 
     @pl.loop(0, QUARTERS)
     def _(step):
-        quarter = lax.rem(mine + 2 * QUARTERS - step - 2, QUARTERS)
+        quarter = lax.rem(mine + QUARTERS - ahead(step), QUARTERS)
 
         @pl.loop(0, size)
         def _(offset):
@@ -269,7 +339,7 @@
 
     @pl.loop(0, QUARTERS)
     def _(step):
-        quarter = lax.rem(mine + step + 2, QUARTERS)
+        quarter = lax.rem(mine + ahead(step), QUARTERS)
 
         @pl.loop(0, size)
         def _(offset):
@@ -283,7 +353,7 @@
         pick = jnp.where(slot == place_col_ref[...], 1.0, 0.0).astype(BF16)
         total[...] += jnp.dot(pick, returned[span(quarter), :], preferred_element_type=F32)
 
-    out_ref[...] = (resid_ref[...].astype(F32) + gate_ref[...] * total[...]).astype(BF16)
+    out_ref[...] = total[...].astype(BF16)
 
     @pl.loop(0, peers)
     def _(target):
@@ -293,7 +363,7 @@
             back(target).wait_send()
 
 
-def expert_layer(position, normed, resid, gate, up_weight, down_weight, slots):
+def expert_layer(place_row, place_col, normed, up_weight, down_weight, slots):
     count, features = normed.shape
     hidden = up_weight.shape[-1]
     peers = lax.axis_size("lon")
@@ -302,7 +372,7 @@
     return pl.pallas_call(
         functools.partial(expert_kernel, peers),
         out_shape=jax.ShapeDtypeStruct((count, features), BF16),
-        in_specs=[vmem] * 5 + [hbm] * 2,
+        in_specs=[vmem] * 3 + [hbm] * 2,
         out_specs=vmem,
         scratch_shapes=[pltpu.VMEM((slots, features), BF16)] * 4
         + [
@@ -316,7 +386,7 @@
             collective_id=1, has_side_effects=True, vmem_limit_bytes=56 * 1024 * 1024
         ),
         name="experts",
-    )(position[None, :], position[:, None], normed, resid, gate, up_weight, down_weight)
+    )(place_row, place_col, normed, up_weight, down_weight)
 
 
 def local(
@@ -333,28 +403,15 @@
 ):
     columns, lat_count, features = tokens.shape
     token_count = columns * lat_count
-    from_next = from_behind(qkv[1:, :SHIFT], "lon", -1)
-    from_prev = from_behind(qkv[1:, columns - SHIFT :], "lon", 1)
     strips = jnp.dot(bias_table, bias_spread(), precision=lax.Precision.HIGHEST).reshape(-1, WIN, 128)
-    resid, normed, gate = front(
-        tokens, qkv, from_prev, from_next, strips, out_weight, norm_gain, router,
-        expert_ids.reshape(token_count, 1),
+    resid, normed, gate, place_col, place_row = front(
+        tokens, qkv, strips, out_weight, norm_gain, router, expert_ids.reshape(token_count, 1), slot_expert
     )
     peers = lax.axis_size("lon")
-    experts = up_weight.shape[0] * peers
-    capacity = 2 * token_count // experts
-    chosen = expert_ids.reshape(-1)
-    expert_range = jnp.arange(experts, dtype=jnp.int32)
-    chosen_hot = chosen[:, None] == expert_range[None, :]
-    slot_of = jnp.sum(
-        jnp.where(slot_expert[None, :] == expert_range[:, None], expert_range[None, :], 0), axis=1
-    )
-    target = jnp.sum(jnp.where(chosen_hot, slot_of[None, :], 0), axis=1)
-    target_hot = (target[:, None] == jnp.arange(peers, dtype=jnp.int32)[None, :]).astype(jnp.int32)
-    earlier = jnp.cumsum(target_hot, axis=0) - target_hot
-    position = target * capacity + jnp.sum(earlier * target_hot, axis=1)
-    blended = expert_layer(position, normed, resid, gate, up_weight, down_weight, peers * capacity)
-    return blended.reshape(columns, lat_count, features)
+    capacity = 2 * token_count // peers
+    gathered = expert_layer(place_row, place_col, normed, up_weight, down_weight, peers * capacity)
+    blended = resid.astype(F32) + gate * gathered.astype(F32)
+    return blended.astype(BF16).reshape(columns, lat_count, features)
 
 
 def solution(mesh):

time: 195 us -> 189 us (0.969)
  waiting for transfers between devices: 8.66 us -> 0 us
  local copies, waits for them, and re-layouts: 11.8 us -> 3.45 us
  Pallas kernels: 166 us -> 174 us
  other arithmetic: 2.23 us -> 5.56 us
    ppermute x2 -> x0, waiting for transfers between devices: 8.66 us -> none  [from_behind(): return lax.ppermute(value, axis, pairs)]
    pallas_call x1, Pallas kernels: 17.9 us -> 25.7 us  [front(): pl.pallas_call(front_kernel, grid=(2 * groups,), in_specs=[pl.BlockSpec(m...]
    unnamed x20 -> x6, local copies, waits for them, and re-layouts: 6.65 us -> 1.18 us
    convert_element_type x1, other arithmetic: 0.01 us -> 3.1 us  [local(): return blended.astype(BF16).reshape(columns, lat_count, features)]
    slice x2 -> x0, local copies, waits for them, and re-layouts: 2.7 us -> none  [the longest x1 2.48 us: local(): from_next = from_behind(qkv[1:, :SHIFT], 'lon', -1)]
  transfers between devices with their start and end apart: 2 -> 0, of which waited for: 2 -> 0; matrix products, arithmetic and copies ran while one was open for 5% -> 0% of each run, Pallas kernels for 0% -> 0%
where the time goes in v3:
time: 189 us; the launch traced here: 185 us
  Pallas kernels  174 us (92%)
  other arithmetic  5.56 us (3%)
  local copies, waits for them, and re-layouts  3.45 us (2%)
    pallas_call x1, Pallas kernels, expert_layer(): pl.pallas_call(functools.partial(expert_kernel, peers), out_shape=jax.Sha...  149 us
    pallas_call x1, Pallas kernels, front(): pl.pallas_call(front_kernel, grid=(2 * groups,), in_specs=[pl.BlockSpec(m...  25.7 us

profile of v3, /device:TPU:9, one launch (start us, length us, event | category | flops | bytes accessed | tf_op | source)
XLA Modules:
  0.0 185.1 jit_solution(6535668362542554889)
XLA Ops:
  0.0 0.0 copy-start
  0.0 1.3 broadcast_in_dim.6.gain_ref
  1.3 0.5 broadcast.4
  1.8 1.4 reduce.4
  3.2 0.0 copy-done
  3.2 1.9 %convolution_bitcast_fusion = f32[3,8,8,128]{3,1,2,0:T(8,128)S(1)} fusion(f32[225,1024]{1,0:T(8,128)} %constant.2.clone, f32[24,225]{1,0:T(8,128)S(1)} %copy-done), kind=kOutput, calls=%fused_computation.1 | convolution fusion | flops 66355200 | bytes 1041504 | tf_op jit(solution)/shard_map/dot_general | solution.py:406
  5.0 0.7 copy.13
  5.7 1.0 reshape.16.chosen_ref
  6.7 25.7 %front.1 = (bf16[512,1536]{1,0:T(8,128)(2,1)}, bf16[512,1536]{1,0:T(8,128)(2,1)}, f32[512,1]{1,0:T(8,128)}, s32[512,1]{1,0:T(8,128)}, s32[1,512]{1,0:T(1,128)}) custom-call(bf16[3,16,32,1536]{3,2,1,0:T(8,128)(2,1)} %v_ref.1, bf16[3,16,32,1536]{3,2,1,0:T(8,128)(2,1)} %v_ref.1, bf16[3,16,32,1536]{3,2,1,0:T(8,128)(2,1)} %v_ref.1, ...), custom_call_target="tpu_custom_call" | custom-call | tf_op jit(solution)/shard_map/front/pallas_call | solution.py:198
  32.3 1.1 reduce.1
  33.4 0.0 copy-start.1
  33.4 148.5 %experts.1 = bf16[512,1536]{1,0:T(8,128)(2,1)} custom-call(s32[1,512]{1,0:T(1,128)} %get-tuple-element.12.place_row_ref, s32[512,1]{1,0:T(8,128)} %get-tuple-element.13.place_col_ref, bf16[512,1536]{1,0:T(8,128)(2,1)} %get-tuple-element.14.normed_ref, bf16[1,1536,1024]{2,1,0:T(8,128)(2,1)} %up_hbm.1, bf16[1,1024,1536]{2,1,0:T(8,128)(2,1)} %down_hbm.1), custom_call_target="tpu_custom_call" | custom-call | tf_op jit(solution)/shard_map/experts/pallas_call | solution.py:372
  182.0 0.0 copy-done.1
  182.0 3.1 %add_convert_fusion = bf16[512,1536]{1,0:T(8,128)(2,1)} fusion(bf16[512,1536]{1,0:T(8,128)(2,1)} %experts.1, bf16[512,1536]{1,0:T(8,128)(2,1)S(1)} %copy-done.1, f32[512]{0:T(512)S(1)} %reduce.1), kind=kLoop, calls=%fused_computation | loop fusion | flops 3932160 | bytes 4720640 | tf_op jit(solution)/shard_map/convert_element_type | solution.py:414
Async XLA Ops:
  0.0 3.2 %copy-start = (f32[24,225]{1,0:T(8,128)S(1)}, f32[24,225]{1,0:T(8,128)}, u32[]{:S(2)}) copy-start(f32[24,225]{1,0:T(8,128)} %param.13) | copy-start | bytes 64804
  33.4 148.6 %copy-start.1 = (bf16[512,1536]{1,0:T(8,128)(2,1)S(1)}, bf16[512,1536]{1,0:T(8,128)(2,1)}, u32[]{:S(2)}) copy-start(bf16[512,1536]{1,0:T(8,128)(2,1)} %get-tuple-element.10) | copy-start | bytes 4718596

commit v4 on v3

--- a/solution.py
+++ b/solution.py
@@ -72,12 +72,14 @@
             )
         pl.semaphore_wait(barrier, 2)
 
-        @pl.loop(0, groups)
-        def _(index):
-            up(index).start()
-            down(index).start()
-
+        up(0).start()
+        down(0).start()
         total[...] = tokens_ref[...].astype(F32)
+
+    @pl.when(step < groups - 1)
+    def _():
+        up(step + 1).start()
+        down(step + 1).start()
 
     heads = []
     for head in range(GROUP):
@@ -156,9 +158,9 @@
 
     @pl.when(step == 1)
     def _():
-        count, experts = chosen_ref.shape[0], slot_ref.shape[1]
+        count, experts = total.shape[0], slot_ref.shape[1]
         cap = 2 * count // experts
-        hot = jnp.where(chosen_ref[...] == slot_ref[...], 1.0, 0.0)
+        hot = jnp.where(chosen_ref[...].reshape(count, 1) == slot_ref[...], 1.0, 0.0)
         row = lax.broadcasted_iota(jnp.int32, (count, count), 0)
         col = lax.broadcasted_iota(jnp.int32, (count, count), 1)
         before = jnp.where(col < row, 1.0, 0.0).astype(BF16)
@@ -174,11 +176,11 @@
         resid_ref[...] = resid
         resid_f = resid.astype(F32)
         scale = lax.rsqrt(jnp.mean(resid_f * resid_f, axis=-1, keepdims=True) + 1e-05)
-        normed = (resid_f * scale * gain_ref[...]).astype(BF16)
+        normed = (resid_f * scale * gain_ref[...].reshape(1, -1)).astype(BF16)
         normed_ref[...] = normed
         logits = lax.dot_general(normed, router_ref[...], (((1,), (1,)), ((), ())), preferred_element_type=F32)
         expert = lax.broadcasted_iota(jnp.int32, logits.shape, 1)
-        picked = jnp.sum(jnp.where(chosen_ref[...] == expert, logits, 0.0), axis=-1, keepdims=True)
+        picked = jnp.sum(jnp.where(chosen_ref[...].reshape(total.shape[0], 1) == expert, logits, 0.0), axis=-1, keepdims=True)
         gate_ref[...] = jax.nn.sigmoid(picked)
 
         @pl.loop(0, groups)
@@ -202,7 +204,7 @@
             pl.BlockSpec(memory_space=pl.ANY), slab(0), slab(1), slab(2),
             pl.BlockSpec((GROUP, WIN, 128), lambda g: (g % groups, 0, 0)),
             pl.BlockSpec((WIDE, features), lambda g: (g % groups, 0)),
-            whole(count, features), whole(1, features), whole(experts, features), whole(count, 1),
+            whole(count, features), whole(features), whole(experts, features), whole(columns, lats, 1),
             whole(1, experts),
         ],
         out_specs=[
@@ -225,7 +227,7 @@
         name="front",
     )(
         qkv, qkv, qkv, qkv, strips, out_weight, tokens.reshape(count, features),
-        norm_gain[None, :], router.T, chosen, slot_expert[None, :],
+        norm_gain, router.T, chosen, slot_expert[None, :],
     )
 
 
@@ -234,7 +236,7 @@
 
 
 def expert_kernel(
-    peers, place_row_ref, place_col_ref, normed_ref, up_hbm, down_hbm, out_ref,
+    peers, place_row_ref, place_col_ref, normed_ref, resid_ref, gate_ref, up_hbm, down_hbm, out_ref,
     outgoing, incoming, answers, returned, total, up, down, load_sem, send_sem, recv_sem, back_sem, home_sem,
 ):
     me = lax.axis_index("lon")
@@ -285,8 +287,7 @@
     load_down.start()
     pl.semaphore_wait(barrier, peers - 1)
 
-    @pl.loop(0, QUARTERS)
-    def _(step):
+    def dispatch(step):
         quarter = lax.rem(mine + ahead(step), QUARTERS)
         slot = quarter * rows + lax.broadcasted_iota(jnp.int32, (rows, count), 0)
         pick = jnp.where(slot == place_row_ref[...], 1.0, 0.0).astype(BF16)
@@ -304,6 +305,10 @@
             def _():
                 incoming[block(me), :] = outgoing[block(me), :]
 
+    @pl.loop(0, 2)
+    def _(step):
+        dispatch(step)
+
     load_up.wait()
     load_down.wait()
 
@@ -319,6 +324,10 @@
             def _():
                 landed(incoming, recv_sem, source).wait_recv()
 
+        @pl.when(step < QUARTERS - 2)
+        def _():
+            dispatch(step + 2)
+
         inputs = incoming[span(quarter), :]
         hidden = jax.nn.gelu(jnp.dot(inputs, up[...], preferred_element_type=F32)).astype(BF16)
         answers[span(quarter), :] = jnp.dot(hidden, down[...], preferred_element_type=F32).astype(BF16)
@@ -353,7 +362,7 @@
         pick = jnp.where(slot == place_col_ref[...], 1.0, 0.0).astype(BF16)
         total[...] += jnp.dot(pick, returned[span(quarter), :], preferred_element_type=F32)
 
-    out_ref[...] = total[...].astype(BF16)
+    out_ref[...] = (resid_ref[...].astype(F32) + gate_ref[...] * total[...]).astype(BF16)
 
     @pl.loop(0, peers)
     def _(target):
@@ -363,7 +372,7 @@
             back(target).wait_send()
 
 
-def expert_layer(place_row, place_col, normed, up_weight, down_weight, slots):
+def expert_layer(place_row, place_col, normed, resid, gate, up_weight, down_weight, slots):
     count, features = normed.shape
     hidden = up_weight.shape[-1]
     peers = lax.axis_size("lon")
@@ -372,7 +381,7 @@
     return pl.pallas_call(
         functools.partial(expert_kernel, peers),
         out_shape=jax.ShapeDtypeStruct((count, features), BF16),
-        in_specs=[vmem] * 3 + [hbm] * 2,
+        in_specs=[vmem] * 5 + [hbm] * 2,
         out_specs=vmem,
         scratch_shapes=[pltpu.VMEM((slots, features), BF16)] * 4
         + [
@@ -386,7 +395,7 @@
             collective_id=1, has_side_effects=True, vmem_limit_bytes=56 * 1024 * 1024
         ),
         name="experts",
-    )(place_row, place_col, normed, up_weight, down_weight)
+    )(place_row, place_col, normed, resid, gate, up_weight, down_weight)
 
 
 def local(
@@ -405,13 +414,12 @@
     token_count = columns * lat_count
     strips = jnp.dot(bias_table, bias_spread(), precision=lax.Precision.HIGHEST).reshape(-1, WIN, 128)
     resid, normed, gate, place_col, place_row = front(
-        tokens, qkv, strips, out_weight, norm_gain, router, expert_ids.reshape(token_count, 1), slot_expert
+        tokens, qkv, strips, out_weight, norm_gain, router, expert_ids, slot_expert
     )
     peers = lax.axis_size("lon")
     capacity = 2 * token_count // peers
-    gathered = expert_layer(place_row, place_col, normed, up_weight, down_weight, peers * capacity)
-    blended = resid.astype(F32) + gate * gathered.astype(F32)
-    return blended.astype(BF16).reshape(columns, lat_count, features)
+    blended = expert_layer(place_row, place_col, normed, resid, gate, up_weight, down_weight, peers * capacity)
+    return blended.reshape(columns, lat_count, features)
 
 
 def solution(mesh):

time: 189 us -> 193 us (1.021); the launches traced: 185 us -> 193 us
  Pallas kernels: 174 us -> 185 us
  other arithmetic: 5.56 us -> 0 us
  local copies, waits for them, and re-layouts: 3.45 us -> 5.65 us
    pallas_call x1, Pallas kernels: 149 us -> 160 us  [expert_layer(): pl.pallas_call(functools.partial(expert_kernel, peers), out_shape=jax.Sha...]
    unnamed x6 -> x5, local copies, waits for them, and re-layouts: 1.18 us -> 5.65 us
    convert_element_type x1 -> x0, other arithmetic: 3.1 us -> none  [local(): return blended.astype(BF16).reshape(columns, lat_count, features)]
where the time goes in v4:
time: 193 us
  Pallas kernels  185 us (96%)
  local copies, waits for them, and re-layouts  5.65 us (3%)
    pallas_call x1, Pallas kernels, expert_layer(): pl.pallas_call(functools.partial(expert_kernel, peers), out_shape=jax.Sha...  160 us
    pallas_call x1, Pallas kernels, front(): pl.pallas_call(front_kernel, grid=(2 * groups,), in_specs=[pl.BlockSpec(m...  25.6 us
    unnamed x5, local copies, waits for them, and re-layouts  5.65 us

profile of v4, /device:TPU:9, one launch (start us, length us, event | category | flops | bytes accessed | tf_op | source)
XLA Modules:
  0.0 192.7 jit_solution(5059723544751457147)
XLA Ops:
  0.0 0.0 copy-start
  0.0 0.7 copy-done
  0.7 1.8 convolution_bitcast_fusion
  2.6 0.7 copy.13
  3.2 1.6 copy.12.chosen_ref
  4.8 25.6 %front.1 = (bf16[512,1536]{1,0:T(8,128)(2,1)}, bf16[512,1536]{1,0:T(8,128)(2,1)}, f32[512,1]{1,0:T(8,128)}, s32[512,1]{1,0:T(8,128)}, s32[1,512]{1,0:T(1,128)}) custom-call(bf16[3,16,32,1536]{3,2,1,0:T(8,128)(2,1)} %v_ref.1, bf16[3,16,32,1536]{3,2,1,0:T(8,128)(2,1)} %v_ref.1, bf16[3,16,32,1536]{3,2,1,0:T(8,128)(2,1)} %v_ref.1, ...), custom_call_target="tpu_custom_call" | custom-call | tf_op jit(solution)/shard_map/front/pallas_call | solution.py:200
  30.5 159.6 %experts.1 = bf16[512,1536]{1,0:T(8,128)(2,1)} custom-call(s32[1,512]{1,0:T(1,128)} %get-tuple-element.10.place_row_ref, s32[512,1]{1,0:T(8,128)} %get-tuple-element.11.place_col_ref, bf16[512,1536]{1,0:T(8,128)(2,1)} %get-tuple-element.12.normed_ref, bf16[512,1536]{1,0:T(8,128)(2,1)} %get-tuple-element.13.resid_ref, f32[512,1]{1,0:T(8,128)} %get-tuple-element.14.gate_ref, ...), custom_call_target="tpu_custom_call" | custom-call | tf_op jit(solution)/shard_map/experts/pallas_call | solution.py:381
  190.1 2.7 %copy.15 = bf16[16,32,1536]{2,1,0:T(8,128)(2,1)} copy(bf16[16,32,1536]{2,1,0:T(8,128)(2,1)} %bitcast.10) | data formatting | bytes 3145728
Async XLA Ops:
  0.0 0.7 copy-start

commit v5 on v4

--- a/solution.py
+++ b/solution.py
@@ -305,7 +305,7 @@
             def _():
                 incoming[block(me), :] = outgoing[block(me), :]
 
-    @pl.loop(0, 2)
+    @pl.loop(0, QUARTERS - 1)
     def _(step):
         dispatch(step)
 
@@ -324,9 +324,9 @@
             def _():
                 landed(incoming, recv_sem, source).wait_recv()
 
-        @pl.when(step < QUARTERS - 2)
+        @pl.when(step == 0)
         def _():
-            dispatch(step + 2)
+            dispatch(QUARTERS - 1)
 
         inputs = incoming[span(quarter), :]
         hidden = jax.nn.gelu(jnp.dot(inputs, up[...], preferred_element_type=F32)).astype(BF16)

time: 193 us -> 186 us (0.964); the launches traced: 193 us -> 182 us
  Pallas kernels: 185 us -> 175 us
    pallas_call x1, Pallas kernels: 160 us -> 149 us  [expert_layer(): pl.pallas_call(functools.partial(expert_kernel, peers), out_shape=jax.Sha...]
where the time goes in v5:
time: 186 us; the launch traced here: 182 us
  Pallas kernels  175 us (94%)
  local copies, waits for them, and re-layouts  5.65 us (3%)
    pallas_call x1, Pallas kernels, expert_layer(): pl.pallas_call(functools.partial(expert_kernel, peers), out_shape=jax.Sha...  149 us
    pallas_call x1, Pallas kernels, front(): pl.pallas_call(front_kernel, grid=(2 * groups,), in_specs=[pl.BlockSpec(m...  25.6 us
    unnamed x5, local copies, waits for them, and re-layouts  5.65 us

profile of v5, /device:TPU:9, one launch (start us, length us, event | category | flops | bytes accessed | tf_op | source)
XLA Modules:
  0.0 182.5 jit_solution(615382268405053942)
XLA Ops:
  0.0 0.0 copy-start
  0.0 0.7 copy-done
  0.7 1.8 %convolution_bitcast_fusion = f32[3,8,8,128]{3,1,2,0:T(8,128)S(1)} fusion(f32[225,1024]{1,0:T(8,128)} %constant.2.clone, f32[24,225]{1,0:T(8,128)S(1)} %copy-done), kind=kOutput, calls=%fused_computation | convolution fusion | flops 66355200 | bytes 1041504 | tf_op jit(solution)/shard_map/dot_general | solution.py:415
  2.6 0.7 copy.13
  3.2 1.6 copy.12.chosen_ref
  4.8 25.6 %front.1 = (bf16[512,1536]{1,0:T(8,128)(2,1)}, bf16[512,1536]{1,0:T(8,128)(2,1)}, f32[512,1]{1,0:T(8,128)}, s32[512,1]{1,0:T(8,128)}, s32[1,512]{1,0:T(1,128)}) custom-call(bf16[3,16,32,1536]{3,2,1,0:T(8,128)(2,1)} %v_ref.1, bf16[3,16,32,1536]{3,2,1,0:T(8,128)(2,1)} %v_ref.1, bf16[3,16,32,1536]{3,2,1,0:T(8,128)(2,1)} %v_ref.1, ...), custom_call_target="tpu_custom_call" | custom-call | tf_op jit(solution)/shard_map/front/pallas_call | solution.py:200
  30.5 149.3 %experts.1 = bf16[512,1536]{1,0:T(8,128)(2,1)} custom-call(s32[1,512]{1,0:T(1,128)} %get-tuple-element.10.place_row_ref, s32[512,1]{1,0:T(8,128)} %get-tuple-element.11.place_col_ref, bf16[512,1536]{1,0:T(8,128)(2,1)} %get-tuple-element.12.normed_ref, bf16[512,1536]{1,0:T(8,128)(2,1)} %get-tuple-element.13.resid_ref, f32[512,1]{1,0:T(8,128)} %get-tuple-element.14.gate_ref, ...), custom_call_target="tpu_custom_call" | custom-call | tf_op jit(solution)/shard_map/experts/pallas_call | solution.py:381
  179.8 2.7 %copy.15 = bf16[16,32,1536]{2,1,0:T(8,128)(2,1)} copy(bf16[16,32,1536]{2,1,0:T(8,128)(2,1)} %bitcast.10) | data formatting | bytes 3145728
Async XLA Ops:
  0.0 0.7 copy-start
